TPU v7x, 256 devices: a whole 4x4x8 slice. The times are simulated.
256 devices in a mesh: dp: 32 (over y, z), tensor: 8 (over x, core).
Axes of the slice: x: 4, y: 4, z: 8, core: 2. Of those that a mesh axis runs over, the one named last changes fastest.
Arguments:
- tokens: bfloat16 [8192, 4096], P('dp', 'tensor'), may hold values from -6 to 6
- grad_out: bfloat16 [8192, 12288], P('dp', 'tensor'), may hold values from -0.0625 to 0.0625
- projector: bfloat16 [4096, 512], replicated, may hold values from -0.09375 to 0.09375
- moment_one: float32 [512, 12288], P('dp', 'tensor'), may hold values from -1.75 to 1.75
- moment_two: float32 [512, 12288], P('dp', 'tensor'), may hold values from 0.1 to 2
- weight: bfloat16 [4096, 12288], P('dp', 'tensor'), may hold values from -0.09375 to 0.09375
- next_tokens: bfloat16 [16384, 4096], P('dp', 'tensor'), may hold values from -6 to 6
Outputs:
- gate_out: bfloat16 [16384, 12288], P('dp', 'tensor')
- new_first: float32 [512, 12288], P('dp', 'tensor')
- new_second: float32 [512, 12288], P('dp', 'tensor')
All inputs are finite; a program needn't handle non-finite values.
Results may differ from a plain program's by a relative error of at most 0.0045.
The roundings to bfloat16 on the way count: a program that leaves them out, or rounds other values in their place, can miss the bound.
Values may be sent and summed in bfloat16 or wider, within the bound.
No kernel may reach another device: no remote copies, remote signals or barrier semaphores. Data moves between devices by JAX's collectives and lax.ppermute only.
A program may use at most 64 MiB of HBM per device.

v0:
```python
import functools

import jax
import jax.numpy as jnp
from jax import lax
from jax.experimental import pallas as pl
from jax.experimental.pallas import tpu as pltpu
from jax.sharding import Mesh, PartitionSpec as P

ADAM_STEP = 100


beta_one = 0.9
beta_two = 0.95
step_size = 0.02
epsilon = 1e-08

SIZES = {"y": 4, "z": 8, "x": 4, "c": 2}
f32, bf16 = jnp.float32, jnp.bfloat16


def shift(block, axis, by):
    size = SIZES[axis]
    return lax.ppermute(block, axis, [(i, (i + by) % size) for i in range(size)])


def both_ways(up, down, axis):
    return shift(up, axis, 1), shift(down, axis, -1)


def relay(below, above, axis):
    half = below.shape[0] // 2
    return both_ways(below[:half], above[half:], axis)


def order_four(axis):
    me = lax.axis_index(axis)
    return [me, (me + 3) % 4, (me + 1) % 4, (me + 2) % 4]


def pick(part, at):
    return lax.dynamic_index_in_dim(part, at, 0, keepdims=False)


together = lax.optimization_barrier


def product_kernel(blocks_ref, mine_ref, other_ref, left_ref, right_ref, out_ref):
    step = pl.program_id(0)
    value = jnp.dot(mine_ref[0], left_ref[...], preferred_element_type=f32)
    value += jnp.dot(other_ref[0], right_ref[...], preferred_element_type=f32)

    @pl.when(step == 0)
    def _():
        out_ref[...] = value

    @pl.when(step > 0)
    def _():
        out_ref[...] += value


def product(mine, other, right, blocks):
    steps, rows, depth = mine.shape
    columns = right.shape[1]
    return pl.pallas_call(
        product_kernel,
        out_shape=jax.ShapeDtypeStruct((rows, columns), f32),
        grid_spec=pltpu.PrefetchScalarGridSpec(
            num_scalar_prefetch=1,
            grid=(steps,),
            in_specs=[
                pl.BlockSpec((1, rows, depth), lambda i, blocks: (i, 0, 0)),
                pl.BlockSpec((1, rows, depth), lambda i, blocks: (i, 0, 0)),
                pl.BlockSpec((depth, columns), lambda i, blocks: (blocks[i], 0)),
                pl.BlockSpec((depth, columns), lambda i, blocks: (blocks[steps + i], 0)),
            ],
            out_specs=pl.BlockSpec((rows, columns), lambda i, blocks: (0, 0)),
        ),
        compiler_params=pltpu.CompilerParams(vmem_limit_bytes=32 << 20),
        cost_estimate=pl.CostEstimate(
            flops=4 * steps * rows * depth * columns,
            bytes_accessed=4 * steps * depth * (rows + columns) + 4 * rows * columns,
            transcendentals=0,
        ),
    )(blocks, mine, other, right, right)


def last_kernel(blocks_ref, mine_ref, other_ref, weight_ref, low_ref, normed_ref, out_ref):
    steps, _, depth = mine_ref.shape
    value = -step_size * jnp.dot(low_ref[...], normed_ref[...], preferred_element_type=f32)
    for i in range(steps):
        for held, at in ((mine_ref, i), (other_ref, steps + i)):
            start = pl.multiple_of(blocks_ref[at] * depth, depth)
            value += jnp.dot(
                held[i], weight_ref[pl.ds(start, depth), :], preferred_element_type=f32
            )
    out_ref[...] = value.astype(bf16)


def last(mine, other, weight, low, normed, blocks):
    steps, rows, depth = mine.shape
    features, columns = weight.shape
    rank, tile = low.shape[1], 256

    def whole(array):
        return pl.BlockSpec(array.shape, lambda j, blocks: (0,) * array.ndim)

    return pl.pallas_call(
        last_kernel,
        out_shape=jax.ShapeDtypeStruct((rows, columns), bf16),
        grid_spec=pltpu.PrefetchScalarGridSpec(
            num_scalar_prefetch=1,
            grid=(columns // tile,),
            in_specs=[
                whole(mine),
                whole(other),
                pl.BlockSpec((features, tile), lambda j, blocks: (0, j)),
                whole(low),
                pl.BlockSpec((rank, tile), lambda j, blocks: (0, j)),
            ],
            out_specs=pl.BlockSpec((rows, tile), lambda j, blocks: (0, j)),
        ),
        compiler_params=pltpu.CompilerParams(vmem_limit_bytes=52 << 20),
        cost_estimate=pl.CostEstimate(
            flops=2 * rows * (features + rank) * columns,
            bytes_accessed=2 * (features * (rows + columns) + rank * columns + rows * columns),
            transcendentals=0,
        ),
    )(blocks, mine, other, weight, low, normed)


def body(tokens, grad_out, projector, moment_one, moment_two, weight, next_tokens):
    rows, width = tokens.shape
    columns = weight.shape[1]
    core = lax.axis_index("c")
    x_places, y_places = order_four("x"), order_four("y")

    def proj_of(x, c):
        return lax.dynamic_slice_in_dim(projector, (2 * x + c) * width, width, 0)

    def part_of(x, block):
        return jnp.dot(block, proj_of(x, core), preferred_element_type=f32)

    gathered = lax.all_gather(weight, ("y", "z"), axis=0, tiled=True)

    below, above = both_ways(tokens, tokens, "x")
    partial = part_of(x_places[0], tokens)
    below, above, partial = together((below, above, partial))

    low, high = relay(below, above, "x")
    partial = partial + part_of(x_places[1], below) + part_of(x_places[2], above)
    low, high, partial = together((low, high, partial))

    partial = partial + part_of(x_places[3], jnp.concatenate([low, high], 0))
    reduced = (partial + shift(partial, "c", 1)).astype(bf16)
    part = lax.dot_general(
        reduced, grad_out, (((0,), (0,)), ((), ())), preferred_element_type=f32
    ).astype(bf16)
    part, next_tokens = together((part, next_tokens))

    part = part.reshape(4, -1, columns)
    half = part.shape[1] // 2
    distant = pick(part, y_places[3])
    low, high = both_ways(distant[:half], distant[half:], "y")
    low, high, next_tokens = together((low, high, next_tokens))

    up, down = pick(part, y_places[2]).astype(f32), pick(part, y_places[1]).astype(f32)
    up = jnp.concatenate([up[:half] + low.astype(f32), up[half:]], 0).astype(bf16)
    down = jnp.concatenate([down[:half], down[half:] + high.astype(f32)], 0).astype(bf16)
    below, above = both_ways(up, down, "y")
    next_below, next_above = both_ways(next_tokens, next_tokens, "x")
    summed = pick(part, y_places[0]).astype(f32) + below.astype(f32) + above.astype(f32)
    summed = summed.astype(bf16).reshape(8, -1, columns)
    summed, next_below, next_above = together((summed, next_below, next_above))

    low_grad = lax.all_to_all(summed, "z", 0, 0)
    next_far = jnp.concatenate(relay(next_below, next_above, "x"), 0)
    low_grad, next_far = together((low_grad, next_far))

    low_grad = jnp.sum(low_grad.astype(f32), 0)
    new_first = beta_one * moment_one + (1.0 - beta_one) * low_grad
    new_second = beta_two * moment_two + (1.0 - beta_two) * low_grad * low_grad
    first_fix = 1.0 - beta_one**ADAM_STEP
    second_fix = 1.0 - beta_two**ADAM_STEP
    normed = (new_first / first_fix / (jnp.sqrt(new_second / second_fix) + epsilon)).astype(bf16)
    normed = lax.all_to_all(jnp.broadcast_to(normed[None], (8, *normed.shape)), "z", 0, 0)
    normed = normed.reshape(-1, columns)
    mine = jnp.stack([next_tokens, next_below, next_above, next_far], 0)
    other = shift(mine, "c", 1)
    normed, other = together((normed, other))

    normed_y = both_ways(normed, normed, "y")
    natural = jnp.stack([2 * x + c for c in (core, 1 - core) for x in x_places])
    low_next = product(mine, other, projector, natural).astype(bf16)
    size = low_next.shape[1] // 4
    low_next = jnp.concatenate(
        [lax.dynamic_slice_in_dim(low_next, y * size, size, 1) for y in y_places], 1
    )
    normed_y, low_next = together((normed_y, low_next))

    normed_far = relay(*normed_y, "y")
    full_normed = jnp.concatenate([normed, *normed_y, *normed_far], 0)
    gate = last(mine, other, gathered, low_next, full_normed, natural)
    return (gate, new_first, new_second)


def solution(mesh):
    split = Mesh(mesh.devices.reshape(4, 8, 4, 2), ("y", "z", "x", "c"))
    both = P(("y", "z"), ("x", "c"))
    return jax.shard_map(
        body,
        mesh=split,
        in_specs=(both, both, P(), both, both, both, both),
        out_specs=(both, both, both),
        check_vma=False,
    )
```

profile of v0, /device:TPU:1, one launch (start us, length us, event | category | flops | bytes accessed | tf_op | source)
XLA Modules:
  0.0 167.3 jit_solution(11631598359167118212)
XLA Ops:
  7.9 2.1 %collective-permute-start = (bf16[256,512]{1,0:T(8,128)(2,1)}, bf16[256,512]{1,0:T(8,128)(2,1)S(1)}, u32[]{:S(2)}, u32[]{:S(2)}) collective-permute-start(bf16[256,512]{1,0:T(8,128)(2,1)} %param.7), channel_id=1, source_target_pairs={{0,2},{2,4},{4,6},{6,0},{1,3},{3,5},{5,7},{7,1},{8,10},{10,12},{12... | collective-permute-start | bytes 786440 | tf_op jit(solution)/shard_map/ppermute | solution.py:24
  12.8 2.4 %collective-permute-done = bf16[256,512]{1,0:T(8,128)(2,1)S(1)} collective-permute-done((bf16[256,512]{1,0:T(8,128)(2,1)}, bf16[256,512]{1,0:T(8,128)(2,1)S(1)}, u32[]{:S(2)}, u32[]{:S(2)}) %collective-permute-start) | collective-permute-done | bytes 262176 | tf_op jit(solution)/shard_map/ppermute | solution.py:24
  23.9 3.3 %collective-permute-start.4 = (f32[256,512]{0,1:T(8,128)S(1)}, f32[256,512]{0,1:T(8,128)S(1)}, u32[]{:S(2)}, u32[]{:S(2)}) collective-permute-start(f32[256,512]{0,1:T(8,128)S(1)} %add.158), channel_id=1, source_target_pairs={{0,1},{1,0},{2,3},{3,2},{4,5},{5,4},{6,7},{7,6},{8,9},{9,8},{10,11... | collective-permute-start | bytes 1572872 | tf_op jit(solution)/shard_map/ppermute | solution.py:24
  32.3 6.7 %collective-permute-done.5 = bf16[64,1536]{1,0:T(8,128)(2,1)S(1)} collective-permute-done((bf16[64,1536]{1,0:T(8,128)(2,1)S(1)}, bf16[64,1536]{1,0:T(8,128)(2,1)S(1)}, u32[]{:S(2)}, u32[]{:S(2)}) %collective-permute-start.5) | collective-permute-done | bytes 196640 | tf_op jit(solution)/shard_map/ppermute | solution.py:24
  41.7 1.9 %collective-permute-start.8 = (bf16[128,1536]{1,0:T(8,128)(2,1)}, bf16[128,1536]{1,0:T(8,128)(2,1)}, u32[]{:S(2)}, u32[]{:S(2)}) collective-permute-start(bf16[128,1536]{1,0:T(8,128)(2,1)} %pad_maximum_fusion.4), channel_id=1, source_target_pairs={{0,192},{64,0},{128,64},{192,128},{1,193},{65,1},{129,65},{193,129... | collective-permute-start | bytes 1179656 | tf_op jit(solution)/shard_map/ppermute | solution.py:24
  43.6 2.7 %collective-permute-start.10 = (bf16[512,512]{1,0:T(8,128)(2,1)}, bf16[512,512]{1,0:T(8,128)(2,1)S(1)}, u32[]{:S(2)}, u32[]{:S(2)}) collective-permute-start(bf16[512,512]{1,0:T(8,128)(2,1)} %param.13), channel_id=1, source_target_pairs={{0,6},{2,0},{4,2},{6,4},{1,7},{3,1},{5,3},{7,5},{8,14},{10,8},{12,... | collective-permute-start | bytes 1572872 | tf_op jit(solution)/shard_map/ppermute | solution.py:24
  46.2 6.5 %collective-permute-done.7 = bf16[128,1536]{1,0:T(8,128)(2,1)} collective-permute-done((bf16[128,1536]{1,0:T(8,128)(2,1)}, bf16[128,1536]{1,0:T(8,128)(2,1)}, u32[]{:S(2)}, u32[]{:S(2)}) %collective-permute-start.7) | collective-permute-done | bytes 393248 | tf_op jit(solution)/shard_map/ppermute | solution.py:24
  52.7 2.0 %fusion.1 = bf16[128,1536]{1,0:T(8,128)(2,1)} fusion(bf16[128,1536]{1,0:T(8,128)(2,1)} %collective-permute-done.8, bf16[128,1536]{1,0:T(8,128)(2,1)} %collective-permute-done.7, bf16[4,128,1536]{2,1,0:T(8,128)(2,1)S(1)} %bitcast.44, s32[]{:T(128)S(6)} %select_n.73), kind=kLoop, calls=%fused_computation.5 | loop fusion | flops 1179648 | bytes 1572868 | tf_op jit(solution)/shard_map/convert_element_type | solution.py:173
  56.4 3.0 %collective-permute-done.9 = bf16[512,512]{1,0:T(8,128)(2,1)S(1)} collective-permute-done((bf16[512,512]{1,0:T(8,128)(2,1)}, bf16[512,512]{1,0:T(8,128)(2,1)S(1)}, u32[]{:S(2)}, u32[]{:S(2)}) %collective-permute-start.9) | collective-permute-done | bytes 524320 | tf_op jit(solution)/shard_map/ppermute | solution.py:24
  59.4 8.2 %all-to-all-start = ((bf16[8,16,1536]{2,1,0:T(8,128)(2,1)}), bf16[8,16,1536]{2,1,0:T(8,128)(2,1)S(1)}, u32[]{:S(2)}, u32[]{:S(2)}) async-start(bf16[8,16,1536]{2,1,0:T(8,128)(2,1)} %bitcast.18), calls=%async_computation | async-start | bytes 786432 | tf_op jit(solution)/shard_map/all_to_all | solution.py:176
  67.8 2.9 %collective-permute-start.12 = (bf16[256,512]{1,0:T(8,128)(2,1)S(1)}, bf16[256,512]{1,0:T(8,128)(2,1)S(1)}, u32[]{:S(2)}, u32[]{:S(2)}) collective-permute-start(bf16[256,512]{1,0:T(8,128)(2,1)S(1)} %slice.79), channel_id=1, source_target_pairs={{0,6},{2,0},{4,2},{6,4},{1,7},{3,1},{5,3},{7,5},{8,14},{10,8},{12,... | collective-permute-start | bytes 786440 | tf_op jit(solution)/shard_map/ppermute | solution.py:24
  70.7 3.9 %collective-permute-done.11 = bf16[256,512]{1,0:T(8,128)(2,1)S(1)} collective-permute-done((bf16[256,512]{1,0:T(8,128)(2,1)S(1)}, bf16[256,512]{1,0:T(8,128)(2,1)S(1)}, u32[]{:S(2)}, u32[]{:S(2)}) %collective-permute-start.11) | collective-permute-done | bytes 262176 | tf_op jit(solution)/shard_map/ppermute | solution.py:24
  74.6 10.7 %all-to-all-done = bf16[8,16,1536]{2,1,0:T(8,128)(2,1)S(1)} async-done(((bf16[8,16,1536]{2,1,0:T(8,128)(2,1)}), bf16[8,16,1536]{2,1,0:T(8,128)(2,1)S(1)}, u32[]{:S(2)}, u32[]{:S(2)}) %all-to-all-start) | async-done | bytes 393248 | tf_op jit(solution)/shard_map/all_to_all | solution.py:176
  87.8 3.5 %collective-permute-start.13 = (bf16[4,512,512]{2,1,0:T(8,128)(2,1)S(1)}, bf16[4,512,512]{2,1,0:T(8,128)(2,1)}, u32[]{:S(2)}, u32[]{:S(2)}) collective-permute-start(bf16[4,512,512]{2,1,0:T(8,128)(2,1)S(1)} %pad_maximum_fusion.mine_ref), channel_id=1, source_target_pairs={{0,1},{1,0},{2,3},{3,2},{4,5},{5,4},{6,7},{7,6},{8,9},{9,8},{10,11... | collective-permute-start | bytes 6291464 | tf_op jit(solution)/shard_map/ppermute | solution.py:24
  92.8 3.5 %all-to-all-start.1 = ((bf16[8,16,1536]{2,1,0:T(8,128)(2,1)}), bf16[8,16,1536]{2,1,0:T(8,128)(2,1)S(1)}, u32[]{:S(2)}, u32[]{:S(2)}) async-start(bf16[8,16,1536]{2,1,0:T(8,128)(2,1)} %broadcast_in_dim.2), calls=%async_computation.1 | async-start | bytes 786432 | tf_op jit(solution)/shard_map/all_to_all | solution.py:186
  96.4 18.9 %all-to-all-done.1 = bf16[8,16,1536]{2,1,0:T(8,128)(2,1)S(1)} async-done(((bf16[8,16,1536]{2,1,0:T(8,128)(2,1)}), bf16[8,16,1536]{2,1,0:T(8,128)(2,1)S(1)}, u32[]{:S(2)}, u32[]{:S(2)}) %all-to-all-start.1) | async-done | bytes 393248 | tf_op jit(solution)/shard_map/all_to_all | solution.py:186
  115.7 2.3 %collective-permute-start.15 = (bf16[128,1536]{1,0:T(8,128)(2,1)S(1)}, bf16[128,1536]{1,0:T(8,128)(2,1)S(1)}, u32[]{:S(2)}, u32[]{:S(2)}) collective-permute-start(bf16[128,1536]{1,0:T(8,128)(2,1)S(1)} %bitcast.47), channel_id=1, source_target_pairs={{0,192},{64,0},{128,64},{192,128},{1,193},{65,1},{129,65},{193,129... | collective-permute-start | bytes 1179656 | tf_op jit(solution)/shard_map/ppermute | solution.py:24
  118.0 2.2 %copy-done.1 = bf16[4096,512]{1,0:T(8,128)(2,1)S(1)} copy-done((bf16[4096,512]{1,0:T(8,128)(2,1)S(1)}, bf16[4096,512]{1,0:T(8,128)(2,1)}, u32[]{:S(2)}) %copy-start.1) | copy-done | bytes 4194328
  120.2 5.1 %shard_map.94 = f32[512,512]{1,0:T(8,128)S(1)} custom-call(s32[8]{0:T(128)S(1)} %stack.50.blocks_ref, bf16[4,512,512]{2,1,0:T(8,128)(2,1)S(1)} %pad_maximum_fusion.mine_ref, bf16[4,512,512]{2,1,0:T(8,128)(2,1)} %collective-permute-done.13.other_ref, bf16[4096,512]{1,0:T(8,128)(2,1)S(1)} %copy-done.1, bf16[4096,512]{1,0:T(8,128)(2,1)S(1)} %copy-done.1), custom_call_target="tpu_custom_call" | custom-call | flops 2147483648 | bytes 9437184 | tf_op jit(solution)/shard_map/pallas_call | solution.py:65
  126.3 2.4 %collective-permute-done.14 = bf16[128,1536]{1,0:T(8,128)(2,1)S(1)} collective-permute-done((bf16[128,1536]{1,0:T(8,128)(2,1)S(1)}, bf16[128,1536]{1,0:T(8,128)(2,1)S(1)}, u32[]{:S(2)}, u32[]{:S(2)}) %collective-permute-start.14) | collective-permute-done | bytes 393248 | tf_op jit(solution)/shard_map/ppermute | solution.py:24
  128.9 2.7 %collective-permute-start.17 = (bf16[64,1536]{1,0:T(8,128)(2,1)S(1)}, bf16[64,1536]{1,0:T(8,128)(2,1)S(1)}, u32[]{:S(2)}, u32[]{:S(2)}) collective-permute-start(bf16[64,1536]{1,0:T(8,128)(2,1)S(1)} %slice.81), channel_id=1, source_target_pairs={{0,192},{64,0},{128,64},{192,128},{1,193},{65,1},{129,65},{193,129... | collective-permute-start | bytes 589832 | tf_op jit(solution)/shard_map/ppermute | solution.py:24
  133.2 2.6 %collective-permute-done.16 = bf16[64,1536]{1,0:T(8,128)(2,1)S(1)} collective-permute-done((bf16[64,1536]{1,0:T(8,128)(2,1)S(1)}, bf16[64,1536]{1,0:T(8,128)(2,1)S(1)}, u32[]{:S(2)}, u32[]{:S(2)}) %collective-permute-start.16) | collective-permute-done | bytes 196640 | tf_op jit(solution)/shard_map/ppermute | solution.py:24
  137.2 9.8 %all-gather.2.cloned.1.call-done.weight_ref = bf16[4096,1536]{1,0:T(8,128)(2,1)} async-done(((bf16[128,1536]{1,0:T(8,128)(2,1)}), bf16[4096,1536]{1,0:T(8,128)(2,1)}) %all-gather.2.cloned.1.call-update) | async-done | bytes 12582928 | tf_op jit(solution)/shard_map/all_gather | solution.py:144
  147.0 13.4 %shard_map.95 = bf16[512,1536]{1,0:T(8,128)(2,1)} custom-call(s32[8]{0:T(128)S(1)} %stack.50.blocks_ref, bf16[4,512,512]{2,1,0:T(8,128)(2,1)} %copy-done.2, bf16[4,512,512]{2,1,0:T(8,128)(2,1)} %collective-permute-done.13.other_ref, bf16[4096,1536]{1,0:T(8,128)(2,1)} %all-gather.2.cloned.1.call-done.weight_ref, ...), custom_call_target="tpu_custom_call" | custom-call | flops 7247757312 | bytes 19922944 | tf_op jit(solution)/shard_map/pallas_call | solution.py:108
  (70 shorter events, 30.3 us)
Async XLA Ops:
  7.2 21.5 %copy-start = (bf16[256,1536]{1,0:T(8,128)(2,1)S(1)}, bf16[256,1536]{1,0:T(8,128)(2,1)}, u32[]{:S(2)}) copy-start(bf16[256,1536]{1,0:T(8,128)(2,1)} %param.8) | copy-start | bytes 2359300
  7.2 139.8 %all-gather.2.cloned.1.call-start = ((), (), s32[]{:S(2)}) async-start(), calls=%async_computation.2 | async-start | bytes 12976128 | tf_op jit(solution)/shard_map/all_gather | solution.py:144
  7.9 7.4 %collective-permute-start = (bf16[256,512]{1,0:T(8,128)(2,1)}, bf16[256,512]{1,0:T(8,128)(2,1)S(1)}, u32[]{:S(2)}, u32[]{:S(2)}) collective-permute-start(bf16[256,512]{1,0:T(8,128)(2,1)} %param.7), channel_id=1, source_target_pairs={{0,2},{2,4},{4,6},{6,0},{1,3},{3,5},{5,7},{7,1},{8,10},{10,12},{12... | collective-permute-start | bytes 786440 | tf_op jit(solution)/shard_map/ppermute | solution.py:24
  10.0 6.7 %collective-permute-start.1 = (bf16[256,512]{1,0:T(8,128)(2,1)}, bf16[256,512]{1,0:T(8,128)(2,1)S(1)}, u32[]{:S(2)}, u32[]{:S(2)}) collective-permute-start(bf16[256,512]{1,0:T(8,128)(2,1)} %param.7), channel_id=1, source_target_pairs={{0,6},{2,0},{4,2},{6,4},{1,7},{3,1},{5,3},{7,5},{8,14},{10,8},{12,... | collective-permute-start | bytes 786440 | tf_op jit(solution)/shard_map/ppermute | solution.py:24
  16.8 5.6 %collective-permute-start.2 = (bf16[128,512]{1,0:T(8,128)(2,1)S(1)}, bf16[128,512]{1,0:T(8,128)(2,1)S(1)}, u32[]{:S(2)}, u32[]{:S(2)}) collective-permute-start(bf16[128,512]{1,0:T(8,128)(2,1)S(1)} %slice.62), channel_id=1, source_target_pairs={{0,2},{2,4},{4,6},{6,0},{1,3},{3,5},{5,7},{7,1},{8,10},{10,12},{12... | collective-permute-start | bytes 393224 | tf_op jit(solution)/shard_map/ppermute | solution.py:24
  18.4 4.0 %collective-permute-start.3 = (bf16[128,512]{1,0:T(8,128)(2,1)S(1)}, bf16[128,512]{1,0:T(8,128)(2,1)S(1)}, u32[]{:S(2)}, u32[]{:S(2)}) collective-permute-start(bf16[128,512]{1,0:T(8,128)(2,1)S(1)} %slice.63), channel_id=1, source_target_pairs={{0,6},{2,0},{4,2},{6,4},{1,7},{3,1},{5,3},{7,5},{8,14},{10,8},{12,... | collective-permute-start | bytes 393224 | tf_op jit(solution)/shard_map/ppermute | solution.py:24
  23.9 4.8 %collective-permute-start.4 = (f32[256,512]{0,1:T(8,128)S(1)}, f32[256,512]{0,1:T(8,128)S(1)}, u32[]{:S(2)}, u32[]{:S(2)}) collective-permute-start(f32[256,512]{0,1:T(8,128)S(1)} %add.158), channel_id=1, source_target_pairs={{0,1},{1,0},{2,3},{3,2},{4,5},{5,4},{6,7},{7,6},{8,9},{9,8},{10,11... | collective-permute-start | bytes 1572872 | tf_op jit(solution)/shard_map/ppermute | solution.py:24
  29.3 9.6 %collective-permute-start.5 = (bf16[64,1536]{1,0:T(8,128)(2,1)S(1)}, bf16[64,1536]{1,0:T(8,128)(2,1)S(1)}, u32[]{:S(2)}, u32[]{:S(2)}) collective-permute-start(bf16[64,1536]{1,0:T(8,128)(2,1)S(1)} %get-tuple-element.52), channel_id=1, source_target_pairs={{0,64},{64,128},{128,192},{192,0},{1,65},{65,129},{129,193},{193,1... | collective-permute-start | bytes 589832 | tf_op jit(solution)/shard_map/ppermute | solution.py:24
  30.7 8.2 %collective-permute-start.6 = (bf16[64,1536]{1,0:T(8,128)(2,1)S(1)}, bf16[64,1536]{1,0:T(8,128)(2,1)S(1)}, u32[]{:S(2)}, u32[]{:S(2)}) collective-permute-start(bf16[64,1536]{1,0:T(8,128)(2,1)S(1)} %get-tuple-element.53), channel_id=1, source_target_pairs={{0,192},{64,0},{128,64},{192,128},{1,193},{65,1},{129,65},{193,129... | collective-permute-start | bytes 589832 | tf_op jit(solution)/shard_map/ppermute | solution.py:24
  39.9 12.8 %collective-permute-start.7 = (bf16[128,1536]{1,0:T(8,128)(2,1)}, bf16[128,1536]{1,0:T(8,128)(2,1)}, u32[]{:S(2)}, u32[]{:S(2)}) collective-permute-start(bf16[128,1536]{1,0:T(8,128)(2,1)} %pad_maximum_fusion.3), channel_id=1, source_target_pairs={{0,64},{64,128},{128,192},{192,0},{1,65},{65,129},{129,193},{193,1... | collective-permute-start | bytes 1179656 | tf_op jit(solution)/shard_map/ppermute | solution.py:24
  41.7 11.0 %collective-permute-start.8 = (bf16[128,1536]{1,0:T(8,128)(2,1)}, bf16[128,1536]{1,0:T(8,128)(2,1)}, u32[]{:S(2)}, u32[]{:S(2)}) collective-permute-start(bf16[128,1536]{1,0:T(8,128)(2,1)} %pad_maximum_fusion.4), channel_id=1, source_target_pairs={{0,192},{64,0},{128,64},{192,128},{1,193},{65,1},{129,65},{193,129... | collective-permute-start | bytes 1179656 | tf_op jit(solution)/shard_map/ppermute | solution.py:24
  43.6 12.8 %collective-permute-start.10 = (bf16[512,512]{1,0:T(8,128)(2,1)}, bf16[512,512]{1,0:T(8,128)(2,1)S(1)}, u32[]{:S(2)}, u32[]{:S(2)}) collective-permute-start(bf16[512,512]{1,0:T(8,128)(2,1)} %param.13), channel_id=1, source_target_pairs={{0,6},{2,0},{4,2},{6,4},{1,7},{3,1},{5,3},{7,5},{8,14},{10,8},{12,... | collective-permute-start | bytes 1572872 | tf_op jit(solution)/shard_map/ppermute | solution.py:24
  46.2 13.2 %collective-permute-start.9 = (bf16[512,512]{1,0:T(8,128)(2,1)}, bf16[512,512]{1,0:T(8,128)(2,1)S(1)}, u32[]{:S(2)}, u32[]{:S(2)}) collective-permute-start(bf16[512,512]{1,0:T(8,128)(2,1)} %param.13), channel_id=1, source_target_pairs={{0,2},{2,4},{4,6},{6,0},{1,3},{3,5},{5,7},{7,1},{8,10},{10,12},{12... | collective-permute-start | bytes 1572872 | tf_op jit(solution)/shard_map/ppermute | solution.py:24
  56.4 28.9 %copy-start.5 = (bf16[512,512]{1,0:T(8,128)(2,1)}, bf16[512,512]{1,0:T(8,128)(2,1)S(1)}, u32[]{:S(2)}) copy-start(bf16[512,512]{1,0:T(8,128)(2,1)S(1)} %collective-permute-done.10) | copy-start | bytes 1572868
  59.4 25.9 %all-to-all-start = ((bf16[8,16,1536]{2,1,0:T(8,128)(2,1)}), bf16[8,16,1536]{2,1,0:T(8,128)(2,1)S(1)}, u32[]{:S(2)}, u32[]{:S(2)}) async-start(bf16[8,16,1536]{2,1,0:T(8,128)(2,1)} %bitcast.18), calls=%async_computation | async-start | bytes 786432 | tf_op jit(solution)/shard_map/all_to_all | solution.py:176
  67.6 6.9 %collective-permute-start.11 = (bf16[256,512]{1,0:T(8,128)(2,1)S(1)}, bf16[256,512]{1,0:T(8,128)(2,1)S(1)}, u32[]{:S(2)}, u32[]{:S(2)}) collective-permute-start(bf16[256,512]{1,0:T(8,128)(2,1)S(1)} %slice.78), channel_id=1, source_target_pairs={{0,2},{2,4},{4,6},{6,0},{1,3},{3,5},{5,7},{7,1},{8,10},{10,12},{12... | collective-permute-start | bytes 786440 | tf_op jit(solution)/shard_map/ppermute | solution.py:24
  67.8 6.8 %collective-permute-start.12 = (bf16[256,512]{1,0:T(8,128)(2,1)S(1)}, bf16[256,512]{1,0:T(8,128)(2,1)S(1)}, u32[]{:S(2)}, u32[]{:S(2)}) collective-permute-start(bf16[256,512]{1,0:T(8,128)(2,1)S(1)} %slice.79), channel_id=1, source_target_pairs={{0,6},{2,0},{4,2},{6,4},{1,7},{3,1},{5,3},{7,5},{8,14},{10,8},{12,... | collective-permute-start | bytes 786440 | tf_op jit(solution)/shard_map/ppermute | solution.py:24
  87.8 37.5 %copy-start.2 = (bf16[4,512,512]{2,1,0:T(8,128)(2,1)}, bf16[4,512,512]{2,1,0:T(8,128)(2,1)S(1)}, u32[]{:S(2)}) copy-start(bf16[4,512,512]{2,1,0:T(8,128)(2,1)S(1)} %pad_maximum_fusion.mine_ref) | copy-start | bytes 6291460
  87.8 27.6 %collective-permute-start.13 = (bf16[4,512,512]{2,1,0:T(8,128)(2,1)S(1)}, bf16[4,512,512]{2,1,0:T(8,128)(2,1)}, u32[]{:S(2)}, u32[]{:S(2)}) collective-permute-start(bf16[4,512,512]{2,1,0:T(8,128)(2,1)S(1)} %pad_maximum_fusion.mine_ref), channel_id=1, source_target_pairs={{0,1},{1,0},{2,3},{3,2},{4,5},{5,4},{6,7},{7,6},{8,9},{9,8},{10,11... | collective-permute-start | bytes 6291464 | tf_op jit(solution)/shard_map/ppermute | solution.py:24
  92.8 22.5 %all-to-all-start.1 = ((bf16[8,16,1536]{2,1,0:T(8,128)(2,1)}), bf16[8,16,1536]{2,1,0:T(8,128)(2,1)S(1)}, u32[]{:S(2)}, u32[]{:S(2)}) async-start(bf16[8,16,1536]{2,1,0:T(8,128)(2,1)} %broadcast_in_dim.2), calls=%async_computation.1 | async-start | bytes 786432 | tf_op jit(solution)/shard_map/all_to_all | solution.py:186
  115.3 13.4 %collective-permute-start.14 = (bf16[128,1536]{1,0:T(8,128)(2,1)S(1)}, bf16[128,1536]{1,0:T(8,128)(2,1)S(1)}, u32[]{:S(2)}, u32[]{:S(2)}) collective-permute-start(bf16[128,1536]{1,0:T(8,128)(2,1)S(1)} %bitcast.46), channel_id=1, source_target_pairs={{0,64},{64,128},{128,192},{192,0},{1,65},{65,129},{129,193},{193,1... | collective-permute-start | bytes 1179656 | tf_op jit(solution)/shard_map/ppermute | solution.py:24
  115.7 13.0 %collective-permute-start.15 = (bf16[128,1536]{1,0:T(8,128)(2,1)S(1)}, bf16[128,1536]{1,0:T(8,128)(2,1)S(1)}, u32[]{:S(2)}, u32[]{:S(2)}) collective-permute-start(bf16[128,1536]{1,0:T(8,128)(2,1)S(1)} %bitcast.47), channel_id=1, source_target_pairs={{0,192},{64,0},{128,64},{192,128},{1,193},{65,1},{129,65},{193,129... | collective-permute-start | bytes 1179656 | tf_op jit(solution)/shard_map/ppermute | solution.py:24
  128.8 7.0 %collective-permute-start.16 = (bf16[64,1536]{1,0:T(8,128)(2,1)S(1)}, bf16[64,1536]{1,0:T(8,128)(2,1)S(1)}, u32[]{:S(2)}, u32[]{:S(2)}) collective-permute-start(bf16[64,1536]{1,0:T(8,128)(2,1)S(1)} %slice.80), channel_id=1, source_target_pairs={{0,64},{64,128},{128,192},{192,0},{1,65},{65,129},{129,193},{193,1... | collective-permute-start | bytes 589832 | tf_op jit(solution)/shard_map/ppermute | solution.py:24
  128.9 7.6 %collective-permute-start.17 = (bf16[64,1536]{1,0:T(8,128)(2,1)S(1)}, bf16[64,1536]{1,0:T(8,128)(2,1)S(1)}, u32[]{:S(2)}, u32[]{:S(2)}) collective-permute-start(bf16[64,1536]{1,0:T(8,128)(2,1)S(1)} %slice.81), channel_id=1, source_target_pairs={{0,192},{64,0},{128,64},{192,128},{1,193},{65,1},{129,65},{193,129... | collective-permute-start | bytes 589832 | tf_op jit(solution)/shard_map/ppermute | solution.py:24
  (6 other events, 33.7 us)
Sparse Core Ops, SparseCore 0:
  10.6 136.3 all-gather.1
where the time goes:
time: 168 us; the launch traced here: 167 us
  waiting for transfers between devices  72.4 us (43%)
  starting transfers between devices  41.7 us (25%)
  Pallas kernels  18.5 us (11%)
  between operations  14.3 us (9%)
  local copies, waits for them, and re-layouts  7.8 us (5%)
  other arithmetic  6.39 us (4%)
  matrix products  6.18 us (4%)
    ppermute x18, waiting for transfers between devices, shift(): lax.ppermute(block, axis, [(i, (i + by) % size) for i in range(size)])  32.2 us
    ppermute x18, starting transfers between devices, shift(): lax.ppermute(block, axis, [(i, (i + by) % size) for i in range(size)])  30 us
    all_to_all x1, waiting for transfers between devices, body(): lax.all_to_all(jnp.broadcast_to(normed[None], (8, *normed.shape)), 'z', 0...  18.9 us
    pallas_call x1, Pallas kernels, last(): pl.pallas_call(last_kernel, out_shape=jax.ShapeDtypeStruct((rows, columns...  13.4 us
    all_to_all x1, waiting for transfers between devices, body(): low_grad = lax.all_to_all(summed, 'z', 0, 0)  10.7 us
    all_gather x1, waiting for transfers between devices, body(): gathered = lax.all_gather(weight, ('y', 'z'), axis=0, tiled=True)  9.84 us
    all_to_all x1, starting transfers between devices, body(): low_grad = lax.all_to_all(summed, 'z', 0, 0)  8.2 us
    unnamed x22, local copies, waits for them, and re-layouts  6.01 us
  transfers between devices with their start and end apart: 21, of which 13 were waited for; matrix products, arithmetic and copies ran while one was open for 10% of the time, Pallas kernels for 3%

commit v1 on v0

v1 whole, which is shorter than its diff:
```python
import functools

import jax
import jax.numpy as jnp
from jax import lax
from jax.experimental import pallas as pl
from jax.experimental.pallas import tpu as pltpu
from jax.sharding import Mesh, PartitionSpec as P

ADAM_STEP = 100


beta_one = 0.9
beta_two = 0.95
step_size = 0.02
epsilon = 1e-08

Y = ("yh", "yl")
SIZES = {Y: 4, "z": 8, "x": 4, "c": 2}
f32, bf16 = jnp.float32, jnp.bfloat16


def shift(block, axis, by):
    size = SIZES[axis]
    return lax.ppermute(block, axis, [(i, (i + by) % size) for i in range(size)])


def both_ways(up, down, axis):
    return shift(up, axis, 1), shift(down, axis, -1)


def relay(below, above, axis):
    half = below.shape[0] // 2
    return both_ways(below[:half], above[half:], axis)


def order_four(axis):
    me = lax.axis_index(axis)
    return [me, (me + 3) % 4, (me + 1) % 4, (me + 2) % 4]


def facing(block):
    return lax.ppermute(block, Y, [(i, 3 - i) for i in range(4)])


def beside(block):
    return lax.ppermute(block, Y, [(i, i ^ 1) for i in range(4)])


def pick(part, at):
    return lax.dynamic_index_in_dim(part, at, 0, keepdims=False)


together = lax.optimization_barrier


def prepare_kernel(blocks_ref, places_ref, *refs):
    pieces, (projector_ref, whole_ref, low_ref, sum_ref) = refs[:-4], refs[-4:]
    step = pl.program_id(0)
    depth = pieces[0].shape[1]
    lanes = 128
    count = depth // lanes

    def put(piece, at):
        for i in range(count):
            start = pl.multiple_of(places_ref[at * count + i] * lanes, lanes)
            whole_ref[:, pl.ds(start, lanes)] = piece[:, i * lanes : (i + 1) * lanes]

    def add(piece, at):
        start = pl.multiple_of(blocks_ref[at] * depth, depth)
        return jnp.dot(
            piece[...], projector_ref[pl.ds(start, depth), :], preferred_element_type=f32
        )

    for side, (own, below, above, low, high) in enumerate((pieces[:5], pieces[5:])):
        for i, piece in enumerate((own, below, above)):
            put(piece, 4 * side + i)
        pl.when(step == 0)(functools.partial(put, low, 4 * side + 3))
        pl.when(step == 1)(functools.partial(put, high, 4 * side + 3))

    @pl.when(step == 0)
    def _():
        sum_ref[...] = add(pieces[0], 0)
        for at, piece in ((1, 1), (2, 2), (3, 3), (4, 5), (5, 6), (6, 7)):
            sum_ref[...] += add(pieces[piece], at)
        low_ref[...] = (sum_ref[...] + add(pieces[8], 7)).astype(bf16)


def prepare(mine, other, projector, blocks, places):
    rows, depth = mine[0].shape[0] // 2, mine[0].shape[1]
    features, rank = projector.shape
    moving = pl.BlockSpec((rows, depth), lambda i, *_: (i, 0))
    fixed = pl.BlockSpec((rows, depth), lambda i, *_: (0, 0))
    return pl.pallas_call(
        prepare_kernel,
        out_shape=(
            jax.ShapeDtypeStruct((2 * rows, features), bf16),
            jax.ShapeDtypeStruct((rows, rank), bf16),
        ),
        grid_spec=pltpu.PrefetchScalarGridSpec(
            num_scalar_prefetch=2,
            grid=(2,),
            in_specs=[moving, moving, moving, fixed, fixed] * 2
            + [pl.BlockSpec((features, rank), lambda i, *_: (0, 0))],
            out_specs=(
                pl.BlockSpec((rows, features), lambda i, *_: (i, 0)),
                pl.BlockSpec((rows, rank), lambda i, *_: (0, 0)),
            ),
            scratch_shapes=[pltpu.VMEM((rows, rank), f32)],
        ),
        compiler_params=pltpu.CompilerParams(vmem_limit_bytes=48 << 20),
        cost_estimate=pl.CostEstimate(
            flops=2 * rows * features * rank,
            bytes_accessed=2 * features * (4 * rows + rank),
            transcendentals=0,
        ),
    )(blocks, places, *mine, *other, projector)


def product_kernel(left_ref, right_ref, out_ref):
    value = jnp.dot(left_ref[...], right_ref[...], preferred_element_type=f32)
    out_ref[...] = value.astype(out_ref.dtype)


def product(left, part, rows, right, dtype):
    features, columns = right.shape
    tile = 256
    return pl.pallas_call(
        product_kernel,
        out_shape=jax.ShapeDtypeStruct((rows, columns), dtype),
        grid=(columns // tile,),
        in_specs=[
            pl.BlockSpec((rows, features), lambda j: (part, 0)),
            pl.BlockSpec((features, tile), lambda j: (0, j)),
        ],
        out_specs=pl.BlockSpec((rows, tile), lambda j: (0, j)),
        compiler_params=pltpu.CompilerParams(vmem_limit_bytes=48 << 20),
        cost_estimate=pl.CostEstimate(
            flops=2 * rows * features * columns,
            bytes_accessed=2 * features * (rows + columns) + 4 * rows * columns,
            transcendentals=0,
        ),
    )(left, right)


def last_kernel(group_ref, own_ref, sent_ref, low_ref, *refs):
    normed, out_ref = jnp.concatenate([ref[...] for ref in refs[:-1]], 0), refs[-1]
    step = pl.program_id(0)
    change = -step_size * jnp.dot(low_ref[...], normed, preferred_element_type=f32)

    @pl.when(step == 0)
    def _():
        out_ref[...] = (own_ref[...] + change).astype(bf16)

    @pl.when(step == 1)
    def _():
        out_ref[...] = (sent_ref[...].astype(f32) + change).astype(bf16)


def last(own, sent, low, normed, group):
    rows, columns = own.shape
    rank = low.shape[1]
    place = lambda j, group: (0, (j + group[0]) % 2)
    fixed = lambda j, group: (0, 0)
    return pl.pallas_call(
        last_kernel,
        out_shape=jax.ShapeDtypeStruct((rows, 2 * columns), bf16),
        grid_spec=pltpu.PrefetchScalarGridSpec(
            num_scalar_prefetch=1,
            grid=(2,),
            in_specs=[
                pl.BlockSpec((rows, columns), fixed),
                pl.BlockSpec((rows, columns), fixed),
                pl.BlockSpec((rows, rank), fixed),
                *[pl.BlockSpec((piece.shape[0], columns), place) for piece in normed],
            ],
            out_specs=pl.BlockSpec((rows, columns), place),
        ),
        compiler_params=pltpu.CompilerParams(vmem_limit_bytes=32 << 20),
        cost_estimate=pl.CostEstimate(
            flops=4 * rows * rank * columns,
            bytes_accessed=10 * rows * columns + 4 * rank * columns,
            transcendentals=0,
        ),
    )(group.reshape(1), own, sent, low, *normed)


def body(tokens, grad_out, projector, moment_one, moment_two, weight, next_tokens):
    width = tokens.shape[1]
    columns = weight.shape[1]
    core = lax.axis_index("c")
    x_places, y_places = order_four("x"), order_four(Y)

    def proj_of(x, c):
        return lax.dynamic_slice_in_dim(projector, (2 * x + c) * width, width, 0)

    def part_of(x, block):
        return jnp.dot(block, proj_of(x, core), preferred_element_type=f32)

    y = lax.axis_index(Y)
    side, group = columns // 2, y // 2
    weight_own = lax.dynamic_slice_in_dim(weight, group * side, side, 1)
    weight_facing = facing(lax.dynamic_slice_in_dim(weight, (1 - group) * side, side, 1))
    below, above = both_ways(tokens, tokens, "x")
    partial = part_of(x_places[0], tokens)
    rows = next_tokens.shape[0]
    below, above, partial, weight_facing = together((below, above, partial, weight_facing))

    weight_pair = jnp.concatenate([weight_own, weight_facing], 0)
    weight_beside = beside(weight_pair)
    low, high = relay(below, above, "x")
    facing_next = facing(next_tokens)
    partial = partial + part_of(x_places[1], below) + part_of(x_places[2], above)
    low, high, partial, facing_next, weight_beside = together(
        (low, high, partial, facing_next, weight_beside)
    )

    gathered = lax.all_gather(
        jnp.concatenate([weight_pair, weight_beside], 0), "z", axis=0, tiled=True
    )
    partial = partial + part_of(x_places[3], jnp.concatenate([low, high], 0))
    reduced = (partial + shift(partial, "c", 1)).astype(bf16)
    part = lax.dot_general(
        reduced, grad_out, (((0,), (0,)), ((), ())), preferred_element_type=f32
    ).astype(bf16)
    pair_next = jnp.concatenate([next_tokens, facing_next], 0)
    (part,) = together((part,))

    part = part.reshape(4, -1, columns)
    half = part.shape[1] // 2
    distant = pick(part, y_places[3])
    low, high = both_ways(distant[:half], distant[half:], Y)
    next_below, next_above = both_ways(pair_next, pair_next, "x")
    low, high = together((low, high))

    up, down = pick(part, y_places[2]).astype(f32), pick(part, y_places[1]).astype(f32)
    up = jnp.concatenate([up[:half] + low.astype(f32), up[half:]], 0).astype(bf16)
    down = jnp.concatenate([down[:half], down[half:] + high.astype(f32)], 0).astype(bf16)
    below, above = both_ways(up, down, Y)
    summed = pick(part, y_places[0]).astype(f32) + below.astype(f32) + above.astype(f32)
    (summed,) = together((summed.astype(bf16).reshape(8, -1, columns),))

    low_grad = lax.all_to_all(summed, "z", 0, 0)
    next_low, next_high = relay(next_below, next_above, "x")
    low_grad, next_low, next_high = together((low_grad, next_low, next_high))

    low_grad = jnp.sum(low_grad.astype(f32), 0)
    new_first = beta_one * moment_one + (1.0 - beta_one) * low_grad
    new_second = beta_two * moment_two + (1.0 - beta_two) * low_grad * low_grad
    first_fix = 1.0 - beta_one**ADAM_STEP
    second_fix = 1.0 - beta_two**ADAM_STEP
    normed = (new_first / first_fix / (jnp.sqrt(new_second / second_fix) + epsilon)).astype(bf16)
    normed = lax.all_to_all(jnp.broadcast_to(normed[None], (8, *normed.shape)), "z", 0, 0)
    normed = normed.reshape(-1, columns)
    mine = [pair_next, next_below, next_above, next_low, next_high]
    other = [shift(piece, "c", 1) for piece in mine]
    blocks = [(x, c) for c in (core, 1 - core) for x in x_places]
    natural = jnp.stack([2 * x + c for x, c in blocks])
    gathered_at = []
    for x, c in blocks:
        place = jnp.where(x == y, 0, jnp.where(x == 3 - y, 1, jnp.where(x == y ^ 1, 2, 3)))
        gathered_at += [4 * (4 * c + i) + place for i in range(4)]
    full_next, low_next = prepare(mine, other, projector, natural, jnp.stack(gathered_at))
    size = low_next.shape[1] // 4
    low_next = jnp.concatenate(
        [lax.dynamic_slice_in_dim(low_next, place * size, size, 1) for place in (y, y ^ 1, 3 - y, 3 - (y ^ 1))],
        1,
    )
    normed, full_next, low_next = together((normed, full_next, low_next))

    normed_beside, normed_facing = beside(normed), facing(normed)
    sent = product(full_next, 1, rows, gathered, bf16)
    normed_beside, normed_facing, sent, full_next = together(
        (normed_beside, normed_facing, sent, full_next)
    )

    sent = facing(sent)
    normed_far = beside(normed_facing)
    own = product(full_next, 0, rows, gathered, f32)
    pieces = (normed, normed_beside, normed_facing, normed_far)
    gate = last(own, sent, low_next, pieces, group)
    return (gate, new_first, new_second)


def solution(mesh):
    split = Mesh(mesh.devices.reshape(2, 2, 8, 4, 2), (*Y, "z", "x", "c"))
    both = P((*Y, "z"), ("x", "c"))
    return jax.shard_map(
        body,
        mesh=split,
        in_specs=(both, both, P(), both, both, both, both),
        out_specs=(both, both, both),
        check_vma=False,
    )
```

time: 168 us -> 163 us (0.970)
  waiting for transfers between devices: 72.4 us -> 57.4 us
  Pallas kernels: 18.5 us -> 28.5 us
  starting transfers between devices: 41.7 us -> 46.7 us
  local copies, waits for them, and re-layouts: 7.8 us -> 4.7 us
    ppermute x0 -> x7, waiting for transfers between devices: none -> 17.3 us  [the longest x4 14.4 us: facing(): return lax.ppermute(block, Y, [(i, 3 - i) for i in range(4)])]
    ppermute x18, waiting for transfers between devices: 32.2 us -> 17.9 us  [shift(): lax.ppermute(block, axis, [(i, (i + by) % size) for i in range(size)])]
    all_to_all x1, waiting for transfers between devices: 18.9 us -> 7.35 us  [body(): lax.all_to_all(jnp.broadcast_to(normed[None], (8, *normed.shape)), 'z', 0...]
    pallas_call x1 -> x2, Pallas kernels: 5.07 us -> 14 us  [product(): pl.pallas_call(product_kernel, out_shape=jax.ShapeDtypeStruct((rows, colu...]
    ppermute x0 -> x7, starting transfers between devices: none -> 8.87 us  [the longest x4 7.56 us: facing(): return lax.ppermute(block, Y, [(i, 3 - i) for i in range(4)])]
    all_to_all x1, waiting for transfers between devices: 10.7 us -> 3.49 us  [body(): low_grad = lax.all_to_all(summed, 'z', 0, 0)]
    unnamed x22 -> x15, local copies, waits for them, and re-layouts: 6.01 us -> 1.6 us
    ppermute x18, starting transfers between devices: 30 us -> 26.3 us  [shift(): lax.ppermute(block, axis, [(i, (i + by) % size) for i in range(size)])]
  transfers between devices with their start and end apart: 21 -> 28, of which waited for: 13 -> 12; matrix products, arithmetic and copies ran while one was open for 10% -> 9% of each run, Pallas kernels for 3% -> 15%
where the time goes in v1:
time: 163 us
  waiting for transfers between devices  57.4 us (35%)
  starting transfers between devices  46.7 us (29%)
  Pallas kernels  28.5 us (17%)
  between operations  14.3 us (9%)
  matrix products  6.18 us (4%)
  other arithmetic  4.96 us (3%)
  local copies, waits for them, and re-layouts  4.7 us (3%)
    ppermute x18, starting transfers between devices, shift(): lax.ppermute(block, axis, [(i, (i + by) % size) for i in range(size)])  26.3 us
    ppermute x18, waiting for transfers between devices, shift(): lax.ppermute(block, axis, [(i, (i + by) % size) for i in range(size)])  17.9 us
    ppermute x4, waiting for transfers between devices, facing(): return lax.ppermute(block, Y, [(i, 3 - i) for i in range(4)])  14.4 us
    pallas_call x2, Pallas kernels, product(): pl.pallas_call(product_kernel, out_shape=jax.ShapeDtypeStruct((rows, colu...  14 us
    all_gather x1, waiting for transfers between devices, body(): lax.all_gather(jnp.concatenate([weight_pair, weight_beside], 0), 'z', axi...  11.3 us
    pallas_call x1, Pallas kernels, prepare(): pl.pallas_call(prepare_kernel, out_shape=(jax.ShapeDtypeStruct((2 * rows,...  11.1 us
    all_to_all x1, starting transfers between devices, body(): low_grad = lax.all_to_all(summed, 'z', 0, 0)  7.77 us
    ppermute x4, starting transfers between devices, facing(): return lax.ppermute(block, Y, [(i, 3 - i) for i in range(4)])  7.56 us
  transfers between devices with their start and end apart: 28, of which 12 were waited for; matrix products, arithmetic and copies ran while one was open for 9% of the time, Pallas kernels for 15%

profile of v1, /device:TPU:1, one launch (start us, length us, event | category | flops | bytes accessed | tf_op | source)
XLA Modules:
  0.0 162.7 jit_solution(7339291056284818130)
XLA Ops:
  11.8 2.9 %collective-permute-start.2 = (bf16[128,768]{1,0:T(8,128)(2,1)S(1)}, bf16[128,768]{1,0:T(8,128)(2,1)S(1)}, u32[]{:S(2)}, u32[]{:S(2)}) collective-permute-start(bf16[128,768]{1,0:T(8,128)(2,1)S(1)} %get-tuple-element.63), channel_id=1, source_target_pairs={{0,192},{64,128},{128,64},{192,0},{1,193},{65,129},{129,65},{193,1... | collective-permute-start | bytes 589832 | tf_op jit(solution)/shard_map/ppermute | solution.py:43
  19.1 2.2 %collective-permute-start.4 = (bf16[128,512]{1,0:T(8,128)(2,1)S(1)}, bf16[128,512]{1,0:T(8,128)(2,1)S(1)}, u32[]{:S(2)}, u32[]{:S(2)}) collective-permute-start(bf16[128,512]{1,0:T(8,128)(2,1)S(1)} %slice.57), channel_id=1, source_target_pairs={{0,6},{2,0},{4,2},{6,4},{1,7},{3,1},{5,3},{7,5},{8,14},{10,8},{12,... | collective-permute-start | bytes 393224 | tf_op jit(solution)/shard_map/ppermute | solution.py:25
  24.2 5.4 %collective-permute-done.5 = bf16[512,512]{1,0:T(8,128)(2,1)S(1)} collective-permute-done((bf16[512,512]{1,0:T(8,128)(2,1)}, bf16[512,512]{1,0:T(8,128)(2,1)S(1)}, u32[]{:S(2)}, u32[]{:S(2)}) %collective-permute-start.5) | collective-permute-done | bytes 524320 | tf_op jit(solution)/shard_map/ppermute | solution.py:43
  32.1 3.0 %collective-permute-start.7 = (f32[256,512]{0,1:T(8,128)S(1)}, f32[256,512]{0,1:T(8,128)S(1)}, u32[]{:S(2)}, u32[]{:S(2)}) collective-permute-start(f32[256,512]{0,1:T(8,128)S(1)} %add.300), channel_id=1, source_target_pairs={{0,1},{1,0},{2,3},{3,2},{4,5},{5,4},{6,7},{7,6},{8,9},{9,8},{10,11... | collective-permute-start | bytes 1572872 | tf_op jit(solution)/shard_map/ppermute | solution.py:25
  37.4 2.7 %collective-permute-start.9 = (bf16[64,1536]{1,0:T(8,128)(2,1)S(1)}, bf16[64,1536]{1,0:T(8,128)(2,1)S(1)}, u32[]{:S(2)}, u32[]{:S(2)}) collective-permute-start(bf16[64,1536]{1,0:T(8,128)(2,1)S(1)} %get-tuple-element.57), channel_id=1, source_target_pairs={{0,192},{64,0},{128,64},{192,128},{1,193},{65,1},{129,65},{193,129... | collective-permute-start | bytes 589832 | tf_op jit(solution)/shard_map/ppermute | solution.py:25
  41.7 2.7 %collective-permute-start.14 = (bf16[1024,512]{1,0:T(8,128)(2,1)}, bf16[1024,512]{1,0:T(8,128)(2,1)S(1)}, u32[]{:S(2)}, u32[]{:S(2)}) collective-permute-start(bf16[1024,512]{1,0:T(8,128)(2,1)} %constant_dynamic-update-slice_fusion.refs_0_), channel_id=1, source_target_pairs={{0,6},{2,0},{4,2},{6,4},{1,7},{3,1},{5,3},{7,5},{8,14},{10,8},{12,... | collective-permute-start | bytes 3145736 | tf_op jit(solution)/shard_map/ppermute | solution.py:25
  45.8 2.6 %collective-permute-start.11 = (bf16[128,1536]{1,0:T(8,128)(2,1)}, bf16[128,1536]{1,0:T(8,128)(2,1)}, u32[]{:S(2)}, u32[]{:S(2)}) collective-permute-start(bf16[128,1536]{1,0:T(8,128)(2,1)} %pad_maximum_fusion.4), channel_id=1, source_target_pairs={{0,192},{64,0},{128,64},{192,128},{1,193},{65,1},{129,65},{193,129... | collective-permute-start | bytes 1179656 | tf_op jit(solution)/shard_map/ppermute | solution.py:25
  48.4 7.3 %collective-permute-done.10 = bf16[128,1536]{1,0:T(8,128)(2,1)} collective-permute-done((bf16[128,1536]{1,0:T(8,128)(2,1)S(1)}, bf16[128,1536]{1,0:T(8,128)(2,1)}, u32[]{:S(2)}, u32[]{:S(2)}) %collective-permute-start.10) | collective-permute-done | bytes 393248 | tf_op jit(solution)/shard_map/ppermute | solution.py:25
  57.8 7.8 %all-to-all-start = ((bf16[8,16,1536]{2,1,0:T(8,128)(2,1)}), bf16[8,16,1536]{2,1,0:T(8,128)(2,1)S(1)}, u32[]{:S(2)}, u32[]{:S(2)}) async-start(bf16[8,16,1536]{2,1,0:T(8,128)(2,1)} %bitcast.77), calls=%async_computation | async-start | bytes 786432 | tf_op jit(solution)/shard_map/all_to_all | solution.py:243
  67.2 2.7 %collective-permute-start.15 = (bf16[512,512]{1,0:T(8,128)(2,1)S(1)}, bf16[512,512]{1,0:T(8,128)(2,1)}, u32[]{:S(2)}, u32[]{:S(2)}) collective-permute-start(bf16[512,512]{1,0:T(8,128)(2,1)S(1)} %slice.77), channel_id=1, source_target_pairs={{0,6},{2,0},{4,2},{6,4},{1,7},{3,1},{5,3},{7,5},{8,14},{10,8},{12,... | collective-permute-start | bytes 1572872 | tf_op jit(solution)/shard_map/ppermute | solution.py:25
  69.9 2.3 %collective-permute-start.16 = (bf16[1024,512]{1,0:T(8,128)(2,1)}, bf16[1024,512]{1,0:T(8,128)(2,1)}, u32[]{:S(2)}, u32[]{:S(2)}) collective-permute-start(bf16[1024,512]{1,0:T(8,128)(2,1)} %constant_dynamic-update-slice_fusion.refs_0_), channel_id=1, source_target_pairs={{0,1},{1,0},{2,3},{3,2},{4,5},{5,4},{6,7},{7,6},{8,9},{9,8},{10,11... | collective-permute-start | bytes 3145736 | tf_op jit(solution)/shard_map/ppermute | solution.py:25
  72.7 7.4 %collective-permute-done.13.refs_3_ = bf16[512,512]{1,0:T(8,128)(2,1)} collective-permute-done((bf16[512,512]{1,0:T(8,128)(2,1)S(1)}, bf16[512,512]{1,0:T(8,128)(2,1)}, u32[]{:S(2)}, u32[]{:S(2)}) %collective-permute-start.13) | collective-permute-done | bytes 524320 | tf_op jit(solution)/shard_map/ppermute | solution.py:25
  80.1 3.5 %all-to-all-done = bf16[8,16,1536]{2,1,0:T(8,128)(2,1)S(1)} async-done(((bf16[8,16,1536]{2,1,0:T(8,128)(2,1)}), bf16[8,16,1536]{2,1,0:T(8,128)(2,1)S(1)}, u32[]{:S(2)}, u32[]{:S(2)}) %all-to-all-start) | async-done | bytes 393248 | tf_op jit(solution)/shard_map/all_to_all | solution.py:243
  83.6 3.2 %collective-permute-start.19 = (bf16[512,512]{1,0:T(8,128)(2,1)}, bf16[512,512]{1,0:T(8,128)(2,1)}, u32[]{:S(2)}, u32[]{:S(2)}) collective-permute-start(bf16[512,512]{1,0:T(8,128)(2,1)} %collective-permute-done.13.refs_3_), channel_id=1, source_target_pairs={{0,1},{1,0},{2,3},{3,2},{4,5},{5,4},{6,7},{7,6},{8,9},{9,8},{10,11... | collective-permute-start | bytes 1572872 | tf_op jit(solution)/shard_map/ppermute | solution.py:25
  88.3 3.7 %all-to-all-start.1 = ((bf16[8,16,1536]{2,1,0:T(8,128)(2,1)}), bf16[8,16,1536]{2,1,0:T(8,128)(2,1)S(1)}, u32[]{:S(2)}, u32[]{:S(2)}) async-start(bf16[8,16,1536]{2,1,0:T(8,128)(2,1)} %broadcast_in_dim.2), calls=%async_computation.1 | async-start | bytes 786432 | tf_op jit(solution)/shard_map/all_to_all | solution.py:253
  92.3 11.1 %shard_map.94 = (bf16[1024,4096]{1,0:T(8,128)(2,1)}, bf16[512,512]{1,0:T(8,128)(2,1)S(1)}) custom-call(s32[8]{0:T(128)S(1)} %stack.134.blocks_ref, s32[32]{0:T(128)S(1)} %stack.167.places_ref, bf16[1024,512]{1,0:T(8,128)(2,1)} %constant_dynamic-update-slice_fusion.refs_0_, bf16[1024,512]{1,0:T(8,128)(2,1)S(1)} %collective-permute-done.12.refs_1_, ...), custom_call_target="tpu_custom_call" | custom-call | flops 2147483648 | bytes 20971520 | tf_op jit(solution)/shard_map/pallas_call | solution.py:94
  103.5 7.3 %all-to-all-done.1 = bf16[8,16,1536]{2,1,0:T(8,128)(2,1)S(1)} async-done(((bf16[8,16,1536]{2,1,0:T(8,128)(2,1)}), bf16[8,16,1536]{2,1,0:T(8,128)(2,1)S(1)}, u32[]{:S(2)}, u32[]{:S(2)}) %all-to-all-start.1) | async-done | bytes 393248 | tf_op jit(solution)/shard_map/all_to_all | solution.py:253
  113.7 11.3 %all-gather.2.cloned.1.call-done.right_ref = bf16[4096,768]{1,0:T(8,128)(2,1)} async-done(((bf16[512,768]{1,0:T(8,128)(2,1)}), bf16[4096,768]{1,0:T(8,128)(2,1)}) %all-gather.2.cloned.1.call-update) | async-done | bytes 6291472 | tf_op jit(solution)/shard_map/all_gather | solution.py:218
  125.1 7.0 %shard_map.95 = bf16[512,768]{1,0:T(8,128)(2,1)S(1)} custom-call(bf16[1024,4096]{1,0:T(8,128)(2,1)} %get-tuple-element.44.left_ref, bf16[4096,768]{1,0:T(8,128)(2,1)} %all-gather.2.cloned.1.call-done.right_ref), custom_call_target="tpu_custom_call" | custom-call | flops 3221225472 | bytes 12058624 | tf_op jit(solution)/shard_map/pallas_call | solution.py:128
  132.8 2.5 %collective-permute-start.23 = (bf16[512,768]{1,0:T(8,128)(2,1)S(1)}, bf16[512,768]{1,0:T(8,128)(2,1)S(1)}, u32[]{:S(2)}, u32[]{:S(2)}) collective-permute-start(bf16[512,768]{1,0:T(8,128)(2,1)S(1)} %shard_map.95), channel_id=1, source_target_pairs={{0,192},{64,128},{128,64},{192,0},{1,193},{65,129},{129,65},{193,1... | collective-permute-start | bytes 2359304 | tf_op jit(solution)/shard_map/ppermute | solution.py:43
  135.3 7.0 %shard_map.96.own_ref = f32[512,768]{1,0:T(8,128)S(1)} custom-call(bf16[1024,4096]{1,0:T(8,128)(2,1)} %get-tuple-element.44.left_ref, bf16[4096,768]{1,0:T(8,128)(2,1)} %all-gather.2.cloned.1.call-done.right_ref), custom_call_target="tpu_custom_call" | custom-call | flops 3221225472 | bytes 12058624 | tf_op jit(solution)/shard_map/pallas_call | solution.py:128
  142.3 2.9 %collective-permute-done.24.refs_3_ = bf16[128,1536]{1,0:T(8,128)(2,1)S(1)} collective-permute-done((bf16[128,1536]{1,0:T(8,128)(2,1)}, bf16[128,1536]{1,0:T(8,128)(2,1)S(1)}, u32[]{:S(2)}, u32[]{:S(2)}) %collective-permute-start.24) | collective-permute-done | bytes 393248 | tf_op jit(solution)/shard_map/ppermute | solution.py:47
  145.2 7.3 %collective-permute-done.23.sent_ref = bf16[512,768]{1,0:T(8,128)(2,1)S(1)} collective-permute-done((bf16[512,768]{1,0:T(8,128)(2,1)S(1)}, bf16[512,768]{1,0:T(8,128)(2,1)S(1)}, u32[]{:S(2)}, u32[]{:S(2)}) %collective-permute-start.23) | collective-permute-done | bytes 786464 | tf_op jit(solution)/shard_map/ppermute | solution.py:43
  152.4 3.4 %shard_map.97 = bf16[512,1536]{1,0:T(8,128)(2,1)} custom-call(s32[1]{0:T(128)} %bitcast.group_ref, f32[512,768]{1,0:T(8,128)S(1)} %shard_map.96.own_ref, bf16[512,768]{1,0:T(8,128)(2,1)S(1)} %collective-permute-done.23.sent_ref, bf16[512,512]{1,0:T(8,128)(2,1)S(1)} %pad_maximum_fusion.1.low_ref, bf16[128,1536]{1,0:T(8,128)(2,1)S(1)} %bitcast.73, ...), custom_call_target="tpu_custom_call" | custom-call | flops 805306368 | bytes 5505024 | tf_op jit(solution)/shard_map/pallas_call | solution.py:165
  (78 shorter events, 29.2 us)
Async XLA Ops:
  7.2 117.9 %all-gather.2.cloned.1.call-start = ((), (), s32[]{:S(2)}) async-start(), calls=%async_computation.2 | async-start | bytes 7077888 | tf_op jit(solution)/shard_map/all_gather | solution.py:218
  7.2 10.7 %collective-permute-start = (bf16[256,512]{1,0:T(8,128)(2,1)}, bf16[256,512]{1,0:T(8,128)(2,1)S(1)}, u32[]{:S(2)}, u32[]{:S(2)}) collective-permute-start(bf16[256,512]{1,0:T(8,128)(2,1)} %param.7), channel_id=1, source_target_pairs={{0,2},{2,4},{4,6},{6,0},{1,3},{3,5},{5,7},{7,1},{8,10},{10,12},{12... | collective-permute-start | bytes 786440 | tf_op jit(solution)/shard_map/ppermute | solution.py:25
  9.3 8.6 %collective-permute-start.1 = (bf16[256,512]{1,0:T(8,128)(2,1)}, bf16[256,512]{1,0:T(8,128)(2,1)S(1)}, u32[]{:S(2)}, u32[]{:S(2)}) collective-permute-start(bf16[256,512]{1,0:T(8,128)(2,1)} %param.7), channel_id=1, source_target_pairs={{0,6},{2,0},{4,2},{6,4},{1,7},{3,1},{5,3},{7,5},{8,14},{10,8},{12,... | collective-permute-start | bytes 786440 | tf_op jit(solution)/shard_map/ppermute | solution.py:25
  11.8 6.2 %collective-permute-start.2 = (bf16[128,768]{1,0:T(8,128)(2,1)S(1)}, bf16[128,768]{1,0:T(8,128)(2,1)S(1)}, u32[]{:S(2)}, u32[]{:S(2)}) collective-permute-start(bf16[128,768]{1,0:T(8,128)(2,1)S(1)} %get-tuple-element.63), channel_id=1, source_target_pairs={{0,192},{64,128},{128,64},{192,0},{1,193},{65,129},{129,65},{193,1... | collective-permute-start | bytes 589832 | tf_op jit(solution)/shard_map/ppermute | solution.py:43
  14.7 15.0 %collective-permute-start.5 = (bf16[512,512]{1,0:T(8,128)(2,1)}, bf16[512,512]{1,0:T(8,128)(2,1)S(1)}, u32[]{:S(2)}, u32[]{:S(2)}) collective-permute-start(bf16[512,512]{1,0:T(8,128)(2,1)} %param.13), channel_id=1, source_target_pairs={{0,192},{64,128},{128,64},{192,0},{1,193},{65,129},{129,65},{193,1... | collective-permute-start | bytes 1572872 | tf_op jit(solution)/shard_map/ppermute | solution.py:43
  18.0 11.7 %collective-permute-start.6 = (bf16[256,768]{1,0:T(8,128)(2,1)S(1)}, bf16[256,768]{1,0:T(8,128)(2,1)S(1)}, u32[]{:S(2)}, u32[]{:S(2)}) collective-permute-start(bf16[256,768]{1,0:T(8,128)(2,1)S(1)} %pad_maximum_fusion.2), channel_id=1, source_target_pairs={{0,64},{64,0},{128,192},{192,128},{1,65},{65,1},{129,193},{193,129... | collective-permute-start | bytes 1179656 | tf_op jit(solution)/shard_map/ppermute | solution.py:47
  37.3 7.4 %collective-permute-start.8 = (bf16[64,1536]{1,0:T(8,128)(2,1)S(1)}, bf16[64,1536]{1,0:T(8,128)(2,1)S(1)}, u32[]{:S(2)}, u32[]{:S(2)}) collective-permute-start(bf16[64,1536]{1,0:T(8,128)(2,1)S(1)} %get-tuple-element.56), channel_id=1, source_target_pairs={{0,64},{64,128},{128,192},{192,0},{1,65},{65,129},{129,193},{193,1... | collective-permute-start | bytes 589832 | tf_op jit(solution)/shard_map/ppermute | solution.py:25
  37.4 7.3 %collective-permute-start.9 = (bf16[64,1536]{1,0:T(8,128)(2,1)S(1)}, bf16[64,1536]{1,0:T(8,128)(2,1)S(1)}, u32[]{:S(2)}, u32[]{:S(2)}) collective-permute-start(bf16[64,1536]{1,0:T(8,128)(2,1)S(1)} %get-tuple-element.57), channel_id=1, source_target_pairs={{0,192},{64,0},{128,64},{192,128},{1,193},{65,1},{129,65},{193,129... | collective-permute-start | bytes 589832 | tf_op jit(solution)/shard_map/ppermute | solution.py:25
  41.7 25.3 %collective-permute-start.12 = (bf16[1024,512]{1,0:T(8,128)(2,1)}, bf16[1024,512]{1,0:T(8,128)(2,1)S(1)}, u32[]{:S(2)}, u32[]{:S(2)}) collective-permute-start(bf16[1024,512]{1,0:T(8,128)(2,1)} %constant_dynamic-update-slice_fusion.refs_0_), channel_id=1, source_target_pairs={{0,2},{2,4},{4,6},{6,0},{1,3},{3,5},{5,7},{7,1},{8,10},{10,12},{12... | collective-permute-start | bytes 3145736 | tf_op jit(solution)/shard_map/ppermute | solution.py:25
  41.7 25.4 %collective-permute-start.14 = (bf16[1024,512]{1,0:T(8,128)(2,1)}, bf16[1024,512]{1,0:T(8,128)(2,1)S(1)}, u32[]{:S(2)}, u32[]{:S(2)}) collective-permute-start(bf16[1024,512]{1,0:T(8,128)(2,1)} %constant_dynamic-update-slice_fusion.refs_0_), channel_id=1, source_target_pairs={{0,6},{2,0},{4,2},{6,4},{1,7},{3,1},{5,3},{7,5},{8,14},{10,8},{12,... | collective-permute-start | bytes 3145736 | tf_op jit(solution)/shard_map/ppermute | solution.py:25
  44.9 10.8 %collective-permute-start.10 = (bf16[128,1536]{1,0:T(8,128)(2,1)S(1)}, bf16[128,1536]{1,0:T(8,128)(2,1)}, u32[]{:S(2)}, u32[]{:S(2)}) collective-permute-start(bf16[128,1536]{1,0:T(8,128)(2,1)S(1)} %pad_maximum_fusion.3), channel_id=1, source_target_pairs={{0,64},{64,128},{128,192},{192,0},{1,65},{65,129},{129,193},{193,1... | collective-permute-start | bytes 1179656 | tf_op jit(solution)/shard_map/ppermute | solution.py:25
  45.8 9.9 %collective-permute-start.11 = (bf16[128,1536]{1,0:T(8,128)(2,1)}, bf16[128,1536]{1,0:T(8,128)(2,1)}, u32[]{:S(2)}, u32[]{:S(2)}) collective-permute-start(bf16[128,1536]{1,0:T(8,128)(2,1)} %pad_maximum_fusion.4), channel_id=1, source_target_pairs={{0,192},{64,0},{128,64},{192,128},{1,193},{65,1},{129,65},{193,129... | collective-permute-start | bytes 1179656 | tf_op jit(solution)/shard_map/ppermute | solution.py:25
  57.8 25.7 %all-to-all-start = ((bf16[8,16,1536]{2,1,0:T(8,128)(2,1)}), bf16[8,16,1536]{2,1,0:T(8,128)(2,1)S(1)}, u32[]{:S(2)}, u32[]{:S(2)}) async-start(bf16[8,16,1536]{2,1,0:T(8,128)(2,1)} %bitcast.77), calls=%async_computation | async-start | bytes 786432 | tf_op jit(solution)/shard_map/all_to_all | solution.py:243
  67.0 13.1 %collective-permute-start.13 = (bf16[512,512]{1,0:T(8,128)(2,1)S(1)}, bf16[512,512]{1,0:T(8,128)(2,1)}, u32[]{:S(2)}, u32[]{:S(2)}) collective-permute-start(bf16[512,512]{1,0:T(8,128)(2,1)S(1)} %slice.76), channel_id=1, source_target_pairs={{0,2},{2,4},{4,6},{6,0},{1,3},{3,5},{5,7},{7,1},{8,10},{10,12},{12... | collective-permute-start | bytes 1572872 | tf_op jit(solution)/shard_map/ppermute | solution.py:25
  67.2 12.9 %collective-permute-start.15 = (bf16[512,512]{1,0:T(8,128)(2,1)S(1)}, bf16[512,512]{1,0:T(8,128)(2,1)}, u32[]{:S(2)}, u32[]{:S(2)}) collective-permute-start(bf16[512,512]{1,0:T(8,128)(2,1)S(1)} %slice.77), channel_id=1, source_target_pairs={{0,6},{2,0},{4,2},{6,4},{1,7},{3,1},{5,3},{7,5},{8,14},{10,8},{12,... | collective-permute-start | bytes 1572872 | tf_op jit(solution)/shard_map/ppermute | solution.py:25
  69.9 22.3 %collective-permute-start.16 = (bf16[1024,512]{1,0:T(8,128)(2,1)}, bf16[1024,512]{1,0:T(8,128)(2,1)}, u32[]{:S(2)}, u32[]{:S(2)}) collective-permute-start(bf16[1024,512]{1,0:T(8,128)(2,1)} %constant_dynamic-update-slice_fusion.refs_0_), channel_id=1, source_target_pairs={{0,1},{1,0},{2,3},{3,2},{4,5},{5,4},{6,7},{7,6},{8,9},{9,8},{10,11... | collective-permute-start | bytes 3145736 | tf_op jit(solution)/shard_map/ppermute | solution.py:25
  72.2 20.0 %collective-permute-start.17 = (bf16[1024,512]{1,0:T(8,128)(2,1)S(1)}, bf16[1024,512]{1,0:T(8,128)(2,1)}, u32[]{:S(2)}, u32[]{:S(2)}) collective-permute-start(bf16[1024,512]{1,0:T(8,128)(2,1)S(1)} %collective-permute-done.12.refs_1_), channel_id=1, source_target_pairs={{0,1},{1,0},{2,3},{3,2},{4,5},{5,4},{6,7},{7,6},{8,9},{9,8},{10,11... | collective-permute-start | bytes 3145736 | tf_op jit(solution)/shard_map/ppermute | solution.py:25
  72.2 20.1 %collective-permute-start.18 = (bf16[1024,512]{1,0:T(8,128)(2,1)S(1)}, bf16[1024,512]{1,0:T(8,128)(2,1)}, u32[]{:S(2)}, u32[]{:S(2)}) collective-permute-start(bf16[1024,512]{1,0:T(8,128)(2,1)S(1)} %collective-permute-done.14.refs_2_), channel_id=1, source_target_pairs={{0,1},{1,0},{2,3},{3,2},{4,5},{5,4},{6,7},{7,6},{8,9},{9,8},{10,11... | collective-permute-start | bytes 3145736 | tf_op jit(solution)/shard_map/ppermute | solution.py:25
  83.6 8.7 %collective-permute-start.19 = (bf16[512,512]{1,0:T(8,128)(2,1)}, bf16[512,512]{1,0:T(8,128)(2,1)}, u32[]{:S(2)}, u32[]{:S(2)}) collective-permute-start(bf16[512,512]{1,0:T(8,128)(2,1)} %collective-permute-done.13.refs_3_), channel_id=1, source_target_pairs={{0,1},{1,0},{2,3},{3,2},{4,5},{5,4},{6,7},{7,6},{8,9},{9,8},{10,11... | collective-permute-start | bytes 1572872 | tf_op jit(solution)/shard_map/ppermute | solution.py:25
  88.3 22.6 %all-to-all-start.1 = ((bf16[8,16,1536]{2,1,0:T(8,128)(2,1)}), bf16[8,16,1536]{2,1,0:T(8,128)(2,1)S(1)}, u32[]{:S(2)}, u32[]{:S(2)}) async-start(bf16[8,16,1536]{2,1,0:T(8,128)(2,1)} %broadcast_in_dim.2), calls=%async_computation.1 | async-start | bytes 786432 | tf_op jit(solution)/shard_map/all_to_all | solution.py:253
  110.9 21.2 %collective-permute-start.21 = (bf16[128,1536]{1,0:T(8,128)(2,1)S(1)}, bf16[128,1536]{1,0:T(8,128)(2,1)S(1)}, u32[]{:S(2)}, u32[]{:S(2)}) collective-permute-start(bf16[128,1536]{1,0:T(8,128)(2,1)S(1)} %bitcast.71), channel_id=1, source_target_pairs={{0,64},{64,0},{128,192},{192,128},{1,65},{65,1},{129,193},{193,129... | collective-permute-start | bytes 1179656 | tf_op jit(solution)/shard_map/ppermute | solution.py:47
  111.7 21.2 %collective-permute-start.22 = (bf16[128,1536]{1,0:T(8,128)(2,1)S(1)}, bf16[128,1536]{1,0:T(8,128)(2,1)}, u32[]{:S(2)}, u32[]{:S(2)}) collective-permute-start(bf16[128,1536]{1,0:T(8,128)(2,1)S(1)} %bitcast.72), channel_id=1, source_target_pairs={{0,192},{64,128},{128,64},{192,0},{1,193},{65,129},{129,65},{193,1... | collective-permute-start | bytes 1179656 | tf_op jit(solution)/shard_map/ppermute | solution.py:43
  132.8 19.6 %collective-permute-start.23 = (bf16[512,768]{1,0:T(8,128)(2,1)S(1)}, bf16[512,768]{1,0:T(8,128)(2,1)S(1)}, u32[]{:S(2)}, u32[]{:S(2)}) collective-permute-start(bf16[512,768]{1,0:T(8,128)(2,1)S(1)} %shard_map.95), channel_id=1, source_target_pairs={{0,192},{64,128},{128,64},{192,0},{1,193},{65,129},{129,65},{193,1... | collective-permute-start | bytes 2359304 | tf_op jit(solution)/shard_map/ppermute | solution.py:43
  135.3 9.9 %collective-permute-start.24 = (bf16[128,1536]{1,0:T(8,128)(2,1)}, bf16[128,1536]{1,0:T(8,128)(2,1)S(1)}, u32[]{:S(2)}, u32[]{:S(2)}) collective-permute-start(bf16[128,1536]{1,0:T(8,128)(2,1)} %collective-permute-done.22.refs_2_), channel_id=1, source_target_pairs={{0,64},{64,0},{128,192},{192,128},{1,65},{65,1},{129,193},{193,129... | collective-permute-start | bytes 1179656 | tf_op jit(solution)/shard_map/ppermute | solution.py:47
  (11 other events, 171.2 us)
Sparse Core Ops, SparseCore 0:
  30.7 94.3 all-gather.1

commit v2 on v1

--- a/solution.py
+++ b/solution.py
@@ -117,72 +117,132 @@
     )(blocks, places, *mine, *other, projector)
 
 
-def product_kernel(left_ref, right_ref, out_ref):
-    value = jnp.dot(left_ref[...], right_ref[...], preferred_element_type=f32)
-    out_ref[...] = value.astype(out_ref.dtype)
-
-
-def product(left, part, rows, right, dtype):
-    features, columns = right.shape
-    tile = 256
+def product_kernel(part_ref, left_ref, one, two, three, four, out_ref, whole_ref):
+    half, lanes = one.shape[-2:]
+    for i, (first, second) in enumerate(((one, two), (three, four))):
+        columns = pl.ds(i * lanes, lanes)
+        whole_ref[:, :half, columns] = first[...].reshape(-1, half, lanes)
+        whole_ref[:, half:, columns] = second[...].reshape(-1, half, lanes)
+    whole = whole_ref[...].reshape(-1, 2 * lanes)
+    out_ref[...] = jnp.dot(left_ref[...], whole, preferred_element_type=f32).astype(out_ref.dtype)
+
+
+def product(left, part, weight, first, tiles, dtype, beside=None):
+    rows, features = left.shape[0] // 2, left.shape[1]
+    places, blocks, half, lanes = weight.shape
+    pairs = blocks // 2 + 1
+
+    def block(at):
+        return pl.BlockSpec((places, 1, half, lanes), lambda j, part: (0, at + 2 * j, 0, 0))
+
+    specs = [block(first), block(first + pairs), block(first + 1), block(first + 1 + pairs)]
+    arrays = [weight] * 4
+    if beside is not None:
+        specs[3] = pl.BlockSpec(beside.shape, lambda j, part: (0, 0, 0))
+        arrays[3] = beside
+    columns = tiles * 2 * lanes
     return pl.pallas_call(
         product_kernel,
         out_shape=jax.ShapeDtypeStruct((rows, columns), dtype),
-        grid=(columns // tile,),
-        in_specs=[
-            pl.BlockSpec((rows, features), lambda j: (part, 0)),
-            pl.BlockSpec((features, tile), lambda j: (0, j)),
-        ],
-        out_specs=pl.BlockSpec((rows, tile), lambda j: (0, j)),
+        grid_spec=pltpu.PrefetchScalarGridSpec(
+            num_scalar_prefetch=1,
+            grid=(tiles,),
+            in_specs=[pl.BlockSpec((rows, features), lambda j, part: (part[0], 0)), *specs],
+            out_specs=pl.BlockSpec((rows, 2 * lanes), lambda j, part: (0, j)),
+            scratch_shapes=[pltpu.VMEM((places, 2 * half, 2 * lanes), bf16)],
+        ),
         compiler_params=pltpu.CompilerParams(vmem_limit_bytes=48 << 20),
         cost_estimate=pl.CostEstimate(
             flops=2 * rows * features * columns,
             bytes_accessed=2 * features * (rows + columns) + 4 * rows * columns,
             transcendentals=0,
         ),
-    )(left, right)
-
-
-def last_kernel(group_ref, own_ref, sent_ref, low_ref, *refs):
-    normed, out_ref = jnp.concatenate([ref[...] for ref in refs[:-1]], 0), refs[-1]
-    step = pl.program_id(0)
-    change = -step_size * jnp.dot(low_ref[...], normed, preferred_element_type=f32)
-
-    @pl.when(step == 0)
+    )(part, left, *arrays)
+
+
+def changed(value, low_ref, pieces, columns):
+    normed = jnp.concatenate([piece[:, columns] for piece in pieces], 0)
+    change = jnp.dot(low_ref[...], normed, preferred_element_type=f32)
+    return (value.astype(f32) - step_size * change).astype(bf16)
+
+
+def most_kernel(group_ref, own_one, own_two, sent_one, low_ref, *refs):
+    pieces, out_ref = refs[:-1], refs[-1]
+    cut = own_one.shape[1]
+    first, second = slice(0, cut), slice(cut, out_ref.shape[1])
+
+    @pl.when(pl.program_id(0) == 0)
     def _():
-        out_ref[...] = (own_ref[...] + change).astype(bf16)
-
-    @pl.when(step == 1)
+        out_ref[:, first] = changed(own_one[...], low_ref, pieces, first)
+        out_ref[:, second] = changed(own_two[...], low_ref, pieces, second)
+
+    @pl.when(pl.program_id(0) == 1)
     def _():
-        out_ref[...] = (sent_ref[...].astype(f32) + change).astype(bf16)
+        out_ref[:, first] = changed(sent_one[...], low_ref, pieces, first)
+
+
+def rest_kernel(group_ref, sent_ref, low_ref, *refs):
+    pieces, out_ref = refs[:-2], refs[-1]
+    out_ref[...] = changed(sent_ref[...], low_ref, pieces, slice(None))
 
 
 def last(own, sent, low, normed, group):
-    rows, columns = own.shape
-    rank = low.shape[1]
+    rows, rank = low.shape
+    cut, rest = own[0].shape[1], own[1].shape[1]
+    columns = cut + rest
     place = lambda j, group: (0, (j + group[0]) % 2)
     fixed = lambda j, group: (0, 0)
-    return pl.pallas_call(
-        last_kernel,
-        out_shape=jax.ShapeDtypeStruct((rows, 2 * columns), bf16),
-        grid_spec=pltpu.PrefetchScalarGridSpec(
-            num_scalar_prefetch=1,
-            grid=(2,),
-            in_specs=[
-                pl.BlockSpec((rows, columns), fixed),
-                pl.BlockSpec((rows, columns), fixed),
-                pl.BlockSpec((rows, rank), fixed),
-                *[pl.BlockSpec((piece.shape[0], columns), place) for piece in normed],
-            ],
-            out_specs=pl.BlockSpec((rows, columns), place),
-        ),
-        compiler_params=pltpu.CompilerParams(vmem_limit_bytes=32 << 20),
-        cost_estimate=pl.CostEstimate(
-            flops=4 * rows * rank * columns,
-            bytes_accessed=10 * rows * columns + 4 * rank * columns,
-            transcendentals=0,
-        ),
-    )(group.reshape(1), own, sent, low, *normed)
+    group = group.reshape(1)
+
+    def call(kernel, grid, in_specs, out_spec, width, aliases, *arrays):
+        return pl.pallas_call(
+            kernel,
+            out_shape=jax.ShapeDtypeStruct((rows, 2 * columns), bf16),
+            grid_spec=pltpu.PrefetchScalarGridSpec(
+                num_scalar_prefetch=1, grid=grid, in_specs=in_specs, out_specs=out_spec
+            ),
+            input_output_aliases=aliases,
+            compiler_params=pltpu.CompilerParams(vmem_limit_bytes=32 << 20),
+            cost_estimate=pl.CostEstimate(
+                flops=2 * rows * rank * width,
+                bytes_accessed=5 * rows * width + 2 * rank * width,
+                transcendentals=0,
+            ),
+        )(group, *arrays)
+
+    most = call(
+        most_kernel,
+        (2,),
+        [
+            *[pl.BlockSpec(array.shape, fixed) for array in (*own, sent[0], low)],
+            *[pl.BlockSpec((piece.shape[0], columns), place) for piece in normed],
+        ],
+        pl.BlockSpec((rows, columns), place),
+        columns + cut,
+        {},
+        *own,
+        sent[0],
+        low,
+        *normed,
+    )
+    at = lambda j, group: (0, (1 - group[0]) * (columns // rest) + cut // rest)
+    return call(
+        rest_kernel,
+        (1,),
+        [
+            pl.BlockSpec(sent[1].shape, fixed),
+            pl.BlockSpec(low.shape, fixed),
+            *[pl.BlockSpec((piece.shape[0], rest), at) for piece in normed],
+            pl.BlockSpec(memory_space=pl.ANY),
+        ],
+        pl.BlockSpec((rows, rest), at),
+        rest,
+        {3 + len(normed): 0},
+        sent[1],
+        low,
+        *normed,
+        most,
+    )
 
 
 def body(tokens, grad_out, projector, moment_one, moment_two, weight, next_tokens):
@@ -199,15 +259,17 @@
 
     y = lax.axis_index(Y)
     side, group = columns // 2, y // 2
-    weight_own = lax.dynamic_slice_in_dim(weight, group * side, side, 1)
-    weight_facing = facing(lax.dynamic_slice_in_dim(weight, (1 - group) * side, side, 1))
+    lanes = 128
+    count = side // lanes
+    blocks = jnp.swapaxes(weight.reshape(-1, 2 * count, lanes), 0, 1)
+    weight_own = lax.dynamic_slice_in_dim(blocks, group * count, count, 0)
+    weight_facing = facing(lax.dynamic_slice_in_dim(blocks, (1 - group) * count, count, 0))
     below, above = both_ways(tokens, tokens, "x")
     partial = part_of(x_places[0], tokens)
-    rows = next_tokens.shape[0]
     below, above, partial, weight_facing = together((below, above, partial, weight_facing))
 
-    weight_pair = jnp.concatenate([weight_own, weight_facing], 0)
-    weight_beside = beside(weight_pair)
+    weight_pair = jnp.concatenate([weight_own, weight_facing], 1)
+    weight_beside = beside(weight_pair[:-1])
     low, high = relay(below, above, "x")
     facing_next = facing(next_tokens)
     partial = partial + part_of(x_places[1], below) + part_of(x_places[2], above)
@@ -215,9 +277,7 @@
         (low, high, partial, facing_next, weight_beside)
     )
 
-    gathered = lax.all_gather(
-        jnp.concatenate([weight_pair, weight_beside], 0), "z", axis=0, tiled=True
-    )
+    gathered = lax.all_gather(jnp.concatenate([weight_pair, weight_beside], 0), "z", axis=0)
     partial = partial + part_of(x_places[3], jnp.concatenate([low, high], 0))
     reduced = (partial + shift(partial, "c", 1)).astype(bf16)
     part = lax.dot_general(
@@ -269,16 +329,26 @@
     normed, full_next, low_next = together((normed, full_next, low_next))
 
     normed_beside, normed_facing = beside(normed), facing(normed)
-    sent = product(full_next, 1, rows, gathered, bf16)
-    normed_beside, normed_facing, sent, full_next = together(
-        (normed_beside, normed_facing, sent, full_next)
-    )
-
-    sent = facing(sent)
+    own_part, sent_part = jnp.zeros(1, jnp.int32), jnp.ones(1, jnp.int32)
+    late = beside(gathered[:, count - 1])
+    tiles = count // 2 - 1
+    sent_one = product(full_next, sent_part, gathered, 0, tiles, bf16)
+    normed_beside, normed_facing, sent_one, full_next = together(
+        (normed_beside, normed_facing, sent_one, full_next)
+    )
+
+    sent_one = facing(sent_one)
     normed_far = beside(normed_facing)
-    own = product(full_next, 0, rows, gathered, f32)
+    own_one = product(full_next, own_part, gathered, 0, tiles, f32)
+    late, own_one, full_next = together((late, own_one, full_next))
+
+    sent_two = product(full_next, sent_part, gathered, count - 2, 1, bf16, late)
+    sent_two, full_next = together((sent_two, full_next))
+
+    sent_two = facing(sent_two)
+    own_two = product(full_next, own_part, gathered, count - 2, 1, f32, late)
     pieces = (normed, normed_beside, normed_facing, normed_far)
-    gate = last(own, sent, low_next, pieces, group)
+    gate = last((own_one, own_two), (sent_one, sent_two), low_next, pieces, group)
     return (gate, new_first, new_second)
 
 

time: 163 us -> 160 us (0.982)
  waiting for transfers between devices: 57.4 us -> 38.6 us
  Pallas kernels: 28.5 us -> 33.9 us
  local copies, waits for them, and re-layouts: 4.7 us -> 9.23 us
  starting transfers between devices: 46.7 us -> 50.5 us
    ppermute x4 -> x5, waiting for transfers between devices: 14.4 us -> 5.79 us  [facing(): return lax.ppermute(block, Y, [(i, 3 - i) for i in range(4)])]
    all_gather x1, waiting for transfers between devices: 11.3 us -> 3.55 us  [body(): lax.all_gather(jnp.concatenate([weight_pair, weight_beside], 0), 'z', axi...]
    pallas_call x2 -> x4, Pallas kernels: 14 us -> 19.5 us  [product(): pl.pallas_call(product_kernel, out_shape=jax.ShapeDtypeStruct((rows, colu...]
    ppermute x3 -> x4, waiting for transfers between devices: 2.87 us -> 0.01 us  [beside(): return lax.ppermute(block, Y, [(i, i ^ 1) for i in range(4)])]
    all_to_all x1, waiting for transfers between devices: 3.49 us -> 5.73 us  [body(): low_grad = lax.all_to_all(summed, 'z', 0, 0)]
    ppermute x4 -> x5, starting transfers between devices: 7.56 us -> 9.8 us  [facing(): return lax.ppermute(block, Y, [(i, 3 - i) for i in range(4)])]
    ppermute x18, waiting for transfers between devices: 17.9 us -> 16.2 us  [shift(): lax.ppermute(block, axis, [(i, (i + by) % size) for i in range(size)])]
    pallas_call x1 -> x2, Pallas kernels: 3.41 us -> 3.23 us  [call(): pl.pallas_call(kernel, out_shape=jax.ShapeDtypeStruct((rows, 2 * columns)...]
  transfers between devices with their start and end apart: 28 -> 30, of which waited for: 12 -> 11; matrix products, arithmetic and copies ran while one was open for 9% -> 12% of each run, Pallas kernels for 15% -> 21%
where the time goes in v2:
time: 160 us; the launch traced here: 159 us
  starting transfers between devices  50.5 us (32%)
  waiting for transfers between devices  38.6 us (24%)
  Pallas kernels  33.9 us (21%)
  between operations  14.5 us (9%)
  local copies, waits for them, and re-layouts  9.23 us (6%)
  matrix products  7.21 us (5%)
  other arithmetic  4.7 us (3%)
    ppermute x18, starting transfers between devices, shift(): lax.ppermute(block, axis, [(i, (i + by) % size) for i in range(size)])  26.3 us
    pallas_call x4, Pallas kernels, product(): pl.pallas_call(product_kernel, out_shape=jax.ShapeDtypeStruct((rows, colu...  19.5 us
    ppermute x18, waiting for transfers between devices, shift(): lax.ppermute(block, axis, [(i, (i + by) % size) for i in range(size)])  16.2 us
    pallas_call x1, Pallas kernels, prepare(): pl.pallas_call(prepare_kernel, out_shape=(jax.ShapeDtypeStruct((2 * rows,...  11.1 us
    ppermute x5, starting transfers between devices, facing(): return lax.ppermute(block, Y, [(i, 3 - i) for i in range(4)])  9.8 us
    all_to_all x1, starting transfers between devices, body(): low_grad = lax.all_to_all(summed, 'z', 0, 0)  8.52 us
    all_to_all x1, waiting for transfers between devices, body(): lax.all_to_all(jnp.broadcast_to(normed[None], (8, *normed.shape)), 'z', 0...  7.28 us
    ppermute x5, waiting for transfers between devices, facing(): return lax.ppermute(block, Y, [(i, 3 - i) for i in range(4)])  5.79 us
  transfers between devices with their start and end apart: 30, of which 11 were waited for; matrix products, arithmetic and copies ran while one was open for 12% of the time, Pallas kernels for 21%

profile of v2, /device:TPU:1, one launch (start us, length us, event | category | flops | bytes accessed | tf_op | source)
XLA Modules:
  0.0 158.6 jit_solution(5570488571156341386)
XLA Ops:
  7.2 2.1 %collective-permute-start = (bf16[256,512]{1,0:T(8,128)(2,1)}, bf16[256,512]{1,0:T(8,128)(2,1)S(1)}, u32[]{:S(2)}, u32[]{:S(2)}) collective-permute-start(bf16[256,512]{1,0:T(8,128)(2,1)} %param.7), channel_id=1, source_target_pairs={{0,2},{2,4},{4,6},{6,0},{1,3},{3,5},{5,7},{7,1},{8,10},{10,12},{12... | collective-permute-start | bytes 786440 | tf_op jit(solution)/shard_map/ppermute | solution.py:25
  12.0 2.9 %collective-permute-start.2 = (bf16[6,128,128]{1,2,0:T(8,128)(2,1)S(1)}, bf16[6,128,128]{1,2,0:T(8,128)(2,1)S(1)}, u32[]{:S(2)}, u32[]{:S(2)}) collective-permute-start(bf16[6,128,128]{1,2,0:T(8,128)(2,1)S(1)} %get-tuple-element.73), channel_id=1, source_target_pairs={{0,192},{64,128},{128,64},{192,0},{1,193},{65,129},{129,65},{193,1... | collective-permute-start | bytes 589832 | tf_op jit(solution)/shard_map/ppermute | solution.py:43
  20.5 2.5 %collective-permute-start.4 = (bf16[128,512]{1,0:T(8,128)(2,1)S(1)}, bf16[128,512]{1,0:T(8,128)(2,1)S(1)}, u32[]{:S(2)}, u32[]{:S(2)}) collective-permute-start(bf16[128,512]{1,0:T(8,128)(2,1)S(1)} %slice.63), channel_id=1, source_target_pairs={{0,6},{2,0},{4,2},{6,4},{1,7},{3,1},{5,3},{7,5},{8,14},{10,8},{12,... | collective-permute-start | bytes 393224 | tf_op jit(solution)/shard_map/ppermute | solution.py:25
  25.6 4.3 %collective-permute-done.5 = bf16[512,512]{1,0:T(8,128)(2,1)S(1)} collective-permute-done((bf16[512,512]{1,0:T(8,128)(2,1)}, bf16[512,512]{1,0:T(8,128)(2,1)S(1)}, u32[]{:S(2)}, u32[]{:S(2)}) %collective-permute-start.5) | collective-permute-done | bytes 524320 | tf_op jit(solution)/shard_map/ppermute | solution.py:43
  33.4 3.0 %collective-permute-start.8 = (f32[256,512]{0,1:T(8,128)S(1)}, f32[256,512]{0,1:T(8,128)}, u32[]{:S(2)}, u32[]{:S(2)}) collective-permute-start(f32[256,512]{0,1:T(8,128)S(1)} %add.300), channel_id=1, source_target_pairs={{0,1},{1,0},{2,3},{3,2},{4,5},{5,4},{6,7},{7,6},{8,9},{9,8},{10,11... | collective-permute-start | bytes 1572872 | tf_op jit(solution)/shard_map/ppermute | solution.py:25
  44.4 2.7 %collective-permute-start.15 = (bf16[1024,512]{1,0:T(8,128)(2,1)}, bf16[1024,512]{1,0:T(8,128)(2,1)}, u32[]{:S(2)}, u32[]{:S(2)}) collective-permute-start(bf16[1024,512]{1,0:T(8,128)(2,1)} %constant_dynamic-update-slice_fusion.refs_0_), channel_id=1, source_target_pairs={{0,6},{2,0},{4,2},{6,4},{1,7},{3,1},{5,3},{7,5},{8,14},{10,8},{12,... | collective-permute-start | bytes 3145736 | tf_op jit(solution)/shard_map/ppermute | solution.py:25
  50.4 2.7 %collective-permute-start.12 = (bf16[128,1536]{1,0:T(8,128)(2,1)}, bf16[128,1536]{1,0:T(8,128)(2,1)}, u32[]{:S(2)}, u32[]{:S(2)}) collective-permute-start(bf16[128,1536]{1,0:T(8,128)(2,1)} %pad_maximum_fusion.3), channel_id=1, source_target_pairs={{0,192},{64,0},{128,64},{192,128},{1,193},{65,1},{129,65},{193,129... | collective-permute-start | bytes 1179656 | tf_op jit(solution)/shard_map/ppermute | solution.py:25
  53.1 7.2 %collective-permute-done.11 = bf16[128,1536]{1,0:T(8,128)(2,1)} collective-permute-done((bf16[128,1536]{1,0:T(8,128)(2,1)}, bf16[128,1536]{1,0:T(8,128)(2,1)}, u32[]{:S(2)}, u32[]{:S(2)}) %collective-permute-start.11) | collective-permute-done | bytes 393248 | tf_op jit(solution)/shard_map/ppermute | solution.py:25
  62.3 8.5 %all-to-all-start = ((bf16[8,16,1536]{2,1,0:T(8,128)(2,1)}), bf16[8,16,1536]{2,1,0:T(8,128)(2,1)S(1)}, u32[]{:S(2)}, u32[]{:S(2)}) async-start(bf16[8,16,1536]{2,1,0:T(8,128)(2,1)} %bitcast.104), calls=%async_computation | async-start | bytes 786432 | tf_op jit(solution)/shard_map/all_to_all | solution.py:303
  72.0 2.7 %collective-permute-start.16 = (bf16[512,512]{1,0:T(8,128)(2,1)S(1)}, bf16[512,512]{1,0:T(8,128)(2,1)S(1)}, u32[]{:S(2)}, u32[]{:S(2)}) collective-permute-start(bf16[512,512]{1,0:T(8,128)(2,1)S(1)} %slice.86), channel_id=1, source_target_pairs={{0,6},{2,0},{4,2},{6,4},{1,7},{3,1},{5,3},{7,5},{8,14},{10,8},{12,... | collective-permute-start | bytes 1572872 | tf_op jit(solution)/shard_map/ppermute | solution.py:25
  74.8 3.2 %collective-permute-start.17 = (bf16[1024,512]{1,0:T(8,128)(2,1)}, bf16[1024,512]{1,0:T(8,128)(2,1)}, u32[]{:S(2)}, u32[]{:S(2)}) collective-permute-start(bf16[1024,512]{1,0:T(8,128)(2,1)} %constant_dynamic-update-slice_fusion.refs_0_), channel_id=1, source_target_pairs={{0,1},{1,0},{2,3},{3,2},{4,5},{5,4},{6,7},{7,6},{8,9},{9,8},{10,11... | collective-permute-start | bytes 3145736 | tf_op jit(solution)/shard_map/ppermute | solution.py:25
  78.5 4.5 %collective-permute-done.14.refs_3_ = bf16[512,512]{1,0:T(8,128)(2,1)S(1)} collective-permute-done((bf16[512,512]{1,0:T(8,128)(2,1)S(1)}, bf16[512,512]{1,0:T(8,128)(2,1)S(1)}, u32[]{:S(2)}, u32[]{:S(2)}) %collective-permute-start.14) | collective-permute-done | bytes 524320 | tf_op jit(solution)/shard_map/ppermute | solution.py:25
  83.0 5.7 %all-to-all-done = bf16[8,16,1536]{2,1,0:T(8,128)(2,1)S(1)} async-done(((bf16[8,16,1536]{2,1,0:T(8,128)(2,1)}), bf16[8,16,1536]{2,1,0:T(8,128)(2,1)S(1)}, u32[]{:S(2)}, u32[]{:S(2)}) %all-to-all-start) | async-done | bytes 393248 | tf_op jit(solution)/shard_map/all_to_all | solution.py:303
  88.8 3.2 %collective-permute-start.20 = (bf16[512,512]{1,0:T(8,128)(2,1)S(1)}, bf16[512,512]{1,0:T(8,128)(2,1)}, u32[]{:S(2)}, u32[]{:S(2)}) collective-permute-start(bf16[512,512]{1,0:T(8,128)(2,1)S(1)} %collective-permute-done.14.refs_3_), channel_id=1, source_target_pairs={{0,1},{1,0},{2,3},{3,2},{4,5},{5,4},{6,7},{7,6},{8,9},{9,8},{10,11... | collective-permute-start | bytes 1572872 | tf_op jit(solution)/shard_map/ppermute | solution.py:25
  93.5 3.5 %all-to-all-start.1 = ((bf16[8,16,1536]{2,1,0:T(8,128)(2,1)}), bf16[8,16,1536]{2,1,0:T(8,128)(2,1)S(1)}, u32[]{:S(2)}, u32[]{:S(2)}) async-start(bf16[8,16,1536]{2,1,0:T(8,128)(2,1)} %broadcast_in_dim.2), calls=%async_computation.1 | async-start | bytes 786432 | tf_op jit(solution)/shard_map/all_to_all | solution.py:313
  97.3 11.1 %shard_map.94 = (bf16[1024,4096]{1,0:T(8,128)(2,1)}, bf16[512,512]{1,0:T(8,128)(2,1)S(1)}) custom-call(s32[8]{0:T(128)S(1)} %stack.134.blocks_ref, s32[32]{0:T(128)S(1)} %stack.167.places_ref, bf16[1024,512]{1,0:T(8,128)(2,1)} %constant_dynamic-update-slice_fusion.refs_0_, bf16[1024,512]{1,0:T(8,128)(2,1)S(1)} %collective-permute-done.13.refs_1_, ...), custom_call_target="tpu_custom_call" | custom-call | flops 2147483648 | bytes 20971520 | tf_op jit(solution)/shard_map/pallas_call | solution.py:94
  108.6 7.3 %all-to-all-done.1 = bf16[8,16,1536]{2,1,0:T(8,128)(2,1)S(1)} async-done(((bf16[8,16,1536]{2,1,0:T(8,128)(2,1)}), bf16[8,16,1536]{2,1,0:T(8,128)(2,1)S(1)}, u32[]{:S(2)}, u32[]{:S(2)}) %all-to-all-start.1) | async-done | bytes 393248 | tf_op jit(solution)/shard_map/all_to_all | solution.py:313
  115.9 3.3 %collective-permute-start.23 = (bf16[128,1536]{1,0:T(8,128)(2,1)S(1)}, bf16[128,1536]{1,0:T(8,128)(2,1)S(1)}, u32[]{:S(2)}, u32[]{:S(2)}) collective-permute-start(bf16[128,1536]{1,0:T(8,128)(2,1)S(1)} %bitcast.82), channel_id=1, source_target_pairs={{0,192},{64,128},{128,64},{192,0},{1,193},{65,129},{129,65},{193,1... | collective-permute-start | bytes 1179656 | tf_op jit(solution)/shard_map/ppermute | solution.py:43
  119.2 3.5 %all-gather.3.cloned.1.call-done = bf16[88,256,128]{2,1,0:T(8,128)(2,1)} async-done(((bf16[11,256,128]{2,1,0:T(8,128)(2,1)}), bf16[88,256,128]{2,1,0:T(8,128)(2,1)}) %all-gather.3.cloned.1.call-update) | async-done | bytes 5767184 | tf_op jit(solution)/shard_map/all_gather | solution.py:280
  125.1 5.7 %shard_map.95 = bf16[512,512]{1,0:T(8,128)(2,1)S(1)} custom-call(s32[1]{0:T(128)} %constant.92.clone.1.part_ref, bf16[1024,4096]{1,0:T(8,128)(2,1)} %get-tuple-element.57.left_ref, bf16[8,11,256,128]{3,2,1,0:T(8,128)(2,1)} %bitcast.86, bf16[8,11,256,128]{3,2,1,0:T(8,128)(2,1)} %bitcast.87, bf16[8,11,256,128]{3,2,1,0:T(8,128)(2,1)} %bitcast.88, ...), custom_call_target="tpu_custom_call" | custom-call | flops 2147483648 | bytes 9437184 | tf_op jit(solution)/shard_map/pallas_call | solution.py:144
  133.1 5.8 %shard_map.96.own_one = f32[512,512]{1,0:T(8,128)S(1)} custom-call(s32[1]{0:T(128)} %constant.100.clone.1.part_ref, bf16[1024,4096]{1,0:T(8,128)(2,1)} %get-tuple-element.57.left_ref, bf16[8,11,256,128]{3,2,1,0:T(8,128)(2,1)} %bitcast.90, bf16[8,11,256,128]{3,2,1,0:T(8,128)(2,1)} %bitcast.91, bf16[8,11,256,128]{3,2,1,0:T(8,128)(2,1)} %bitcast.92, ...), custom_call_target="tpu_custom_call" | custom-call | flops 2147483648 | bytes 9437184 | tf_op jit(solution)/shard_map/pallas_call | solution.py:144
  138.9 4.0 %shard_map.97 = bf16[512,256]{1,0:T(8,128)(2,1)S(1)} custom-call(s32[1]{0:T(128)} %constant.92.clone.1.part_ref, bf16[1024,4096]{1,0:T(8,128)(2,1)} %get-tuple-element.57.left_ref, bf16[8,11,256,128]{3,2,1,0:T(8,128)(2,1)} %bitcast.94, bf16[8,11,256,128]{3,2,1,0:T(8,128)(2,1)} %bitcast.95, bf16[8,11,256,128]{3,2,1,0:T(8,128)(2,1)} %bitcast.96, ...), custom_call_target="tpu_custom_call" | custom-call | flops 1073741824 | bytes 6815744 | tf_op jit(solution)/shard_map/pallas_call | solution.py:144
  144.5 4.0 %shard_map.98.own_two = f32[512,256]{1,0:T(8,128)S(1)} custom-call(s32[1]{0:T(128)} %constant.100.clone.1.part_ref, bf16[1024,4096]{1,0:T(8,128)(2,1)} %get-tuple-element.57.left_ref, bf16[8,11,256,128]{3,2,1,0:T(8,128)(2,1)} %bitcast.97, bf16[8,11,256,128]{3,2,1,0:T(8,128)(2,1)} %bitcast.98, bf16[8,11,256,128]{3,2,1,0:T(8,128)(2,1)} %bitcast.99, ...), custom_call_target="tpu_custom_call" | custom-call | flops 1073741824 | bytes 6815744 | tf_op jit(solution)/shard_map/pallas_call | solution.py:144
  148.5 2.2 %shard_map.99.refs_4_ = bf16[512,1536]{1,0:T(8,128)(2,1)} custom-call(s32[1]{0:T(128)} %bitcast.group_ref, f32[512,512]{1,0:T(8,128)S(1)} %shard_map.96.own_one, f32[512,256]{1,0:T(8,128)S(1)} %shard_map.98.own_two, bf16[512,512]{1,0:T(8,128)(2,1)S(1)} %collective-permute-done.26.sent_one, bf16[512,512]{1,0:T(8,128)(2,1)S(1)} %pad_maximum_fusion.1.low_ref, ...), custom_call_target="tpu_custom_call" | custom-call | flops 671088640 | bytes 4587520 | tf_op jit(solution)/shard_map/pallas_call | solution.py:198
  (84 shorter events, 38.5 us)
Async XLA Ops:
  7.2 115.5 %all-gather.3.cloned.1.call-start = ((), (), s32[]{:S(2)}) async-start(), calls=%async_computation.2 | async-start | bytes 6488064 | tf_op jit(solution)/shard_map/all_gather | solution.py:280
  7.2 10.7 %collective-permute-start = (bf16[256,512]{1,0:T(8,128)(2,1)}, bf16[256,512]{1,0:T(8,128)(2,1)S(1)}, u32[]{:S(2)}, u32[]{:S(2)}) collective-permute-start(bf16[256,512]{1,0:T(8,128)(2,1)} %param.7), channel_id=1, source_target_pairs={{0,2},{2,4},{4,6},{6,0},{1,3},{3,5},{5,7},{7,1},{8,10},{10,12},{12... | collective-permute-start | bytes 786440 | tf_op jit(solution)/shard_map/ppermute | solution.py:25
  9.3 8.6 %collective-permute-start.1 = (bf16[256,512]{1,0:T(8,128)(2,1)}, bf16[256,512]{1,0:T(8,128)(2,1)S(1)}, u32[]{:S(2)}, u32[]{:S(2)}) collective-permute-start(bf16[256,512]{1,0:T(8,128)(2,1)} %param.7), channel_id=1, source_target_pairs={{0,6},{2,0},{4,2},{6,4},{1,7},{3,1},{5,3},{7,5},{8,14},{10,8},{12,... | collective-permute-start | bytes 786440 | tf_op jit(solution)/shard_map/ppermute | solution.py:25
  14.9 15.0 %collective-permute-start.5 = (bf16[512,512]{1,0:T(8,128)(2,1)}, bf16[512,512]{1,0:T(8,128)(2,1)S(1)}, u32[]{:S(2)}, u32[]{:S(2)}) collective-permute-start(bf16[512,512]{1,0:T(8,128)(2,1)} %param.13), channel_id=1, source_target_pairs={{0,192},{64,128},{128,64},{192,0},{1,193},{65,129},{129,65},{193,1... | collective-permute-start | bytes 1572872 | tf_op jit(solution)/shard_map/ppermute | solution.py:43
  18.0 12.6 %collective-permute-start.6 = (bf16[5,256,128]{1,2,0:T(8,128)(2,1)S(1)}, bf16[5,256,128]{1,2,0:T(8,128)(2,1)S(1)}, u32[]{:S(2)}, u32[]{:S(2)}) collective-permute-start(bf16[5,256,128]{1,2,0:T(8,128)(2,1)S(1)} %pad_maximum_fusion.4), channel_id=1, source_target_pairs={{0,64},{64,0},{128,192},{192,128},{1,65},{65,1},{129,193},{193,129... | collective-permute-start | bytes 983048 | tf_op jit(solution)/shard_map/ppermute | solution.py:47
  39.8 7.4 %collective-permute-start.10 = (bf16[64,1536]{1,0:T(8,128)(2,1)S(1)}, bf16[64,1536]{1,0:T(8,128)(2,1)S(1)}, u32[]{:S(2)}, u32[]{:S(2)}) collective-permute-start(bf16[64,1536]{1,0:T(8,128)(2,1)S(1)} %get-tuple-element.67), channel_id=1, source_target_pairs={{0,192},{64,0},{128,64},{192,128},{1,193},{65,1},{129,65},{193,129... | collective-permute-start | bytes 589832 | tf_op jit(solution)/shard_map/ppermute | solution.py:25
  44.4 26.4 %collective-permute-start.13 = (bf16[1024,512]{1,0:T(8,128)(2,1)}, bf16[1024,512]{1,0:T(8,128)(2,1)S(1)}, u32[]{:S(2)}, u32[]{:S(2)}) collective-permute-start(bf16[1024,512]{1,0:T(8,128)(2,1)} %constant_dynamic-update-slice_fusion.refs_0_), channel_id=1, source_target_pairs={{0,2},{2,4},{4,6},{6,0},{1,3},{3,5},{5,7},{7,1},{8,10},{10,12},{12... | collective-permute-start | bytes 3145736 | tf_op jit(solution)/shard_map/ppermute | solution.py:25
  44.4 26.5 %collective-permute-start.15 = (bf16[1024,512]{1,0:T(8,128)(2,1)}, bf16[1024,512]{1,0:T(8,128)(2,1)}, u32[]{:S(2)}, u32[]{:S(2)}) collective-permute-start(bf16[1024,512]{1,0:T(8,128)(2,1)} %constant_dynamic-update-slice_fusion.refs_0_), channel_id=1, source_target_pairs={{0,6},{2,0},{4,2},{6,4},{1,7},{3,1},{5,3},{7,5},{8,14},{10,8},{12,... | collective-permute-start | bytes 3145736 | tf_op jit(solution)/shard_map/ppermute | solution.py:25
  49.6 10.6 %collective-permute-start.11 = (bf16[128,1536]{1,0:T(8,128)(2,1)}, bf16[128,1536]{1,0:T(8,128)(2,1)}, u32[]{:S(2)}, u32[]{:S(2)}) collective-permute-start(bf16[128,1536]{1,0:T(8,128)(2,1)} %pad_maximum_fusion.2), channel_id=1, source_target_pairs={{0,64},{64,128},{128,192},{192,0},{1,65},{65,129},{129,193},{193,1... | collective-permute-start | bytes 1179656 | tf_op jit(solution)/shard_map/ppermute | solution.py:25
  50.4 9.8 %collective-permute-start.12 = (bf16[128,1536]{1,0:T(8,128)(2,1)}, bf16[128,1536]{1,0:T(8,128)(2,1)}, u32[]{:S(2)}, u32[]{:S(2)}) collective-permute-start(bf16[128,1536]{1,0:T(8,128)(2,1)} %pad_maximum_fusion.3), channel_id=1, source_target_pairs={{0,192},{64,0},{128,64},{192,128},{1,193},{65,1},{129,65},{193,129... | collective-permute-start | bytes 1179656 | tf_op jit(solution)/shard_map/ppermute | solution.py:25
  62.3 26.5 %all-to-all-start = ((bf16[8,16,1536]{2,1,0:T(8,128)(2,1)}), bf16[8,16,1536]{2,1,0:T(8,128)(2,1)S(1)}, u32[]{:S(2)}, u32[]{:S(2)}) async-start(bf16[8,16,1536]{2,1,0:T(8,128)(2,1)} %bitcast.104), calls=%async_computation | async-start | bytes 786432 | tf_op jit(solution)/shard_map/all_to_all | solution.py:303
  70.8 12.1 %collective-permute-start.14 = (bf16[512,512]{1,0:T(8,128)(2,1)S(1)}, bf16[512,512]{1,0:T(8,128)(2,1)S(1)}, u32[]{:S(2)}, u32[]{:S(2)}) collective-permute-start(bf16[512,512]{1,0:T(8,128)(2,1)S(1)} %slice.85), channel_id=1, source_target_pairs={{0,2},{2,4},{4,6},{6,0},{1,3},{3,5},{5,7},{7,1},{8,10},{10,12},{12... | collective-permute-start | bytes 1572872 | tf_op jit(solution)/shard_map/ppermute | solution.py:25
  72.0 11.0 %collective-permute-start.16 = (bf16[512,512]{1,0:T(8,128)(2,1)S(1)}, bf16[512,512]{1,0:T(8,128)(2,1)S(1)}, u32[]{:S(2)}, u32[]{:S(2)}) collective-permute-start(bf16[512,512]{1,0:T(8,128)(2,1)S(1)} %slice.86), channel_id=1, source_target_pairs={{0,6},{2,0},{4,2},{6,4},{1,7},{3,1},{5,3},{7,5},{8,14},{10,8},{12,... | collective-permute-start | bytes 1572872 | tf_op jit(solution)/shard_map/ppermute | solution.py:25
  74.8 22.5 %collective-permute-start.17 = (bf16[1024,512]{1,0:T(8,128)(2,1)}, bf16[1024,512]{1,0:T(8,128)(2,1)}, u32[]{:S(2)}, u32[]{:S(2)}) collective-permute-start(bf16[1024,512]{1,0:T(8,128)(2,1)} %constant_dynamic-update-slice_fusion.refs_0_), channel_id=1, source_target_pairs={{0,1},{1,0},{2,3},{3,2},{4,5},{5,4},{6,7},{7,6},{8,9},{9,8},{10,11... | collective-permute-start | bytes 3145736 | tf_op jit(solution)/shard_map/ppermute | solution.py:25
  78.0 19.3 %collective-permute-start.18 = (bf16[1024,512]{1,0:T(8,128)(2,1)S(1)}, bf16[1024,512]{1,0:T(8,128)(2,1)}, u32[]{:S(2)}, u32[]{:S(2)}) collective-permute-start(bf16[1024,512]{1,0:T(8,128)(2,1)S(1)} %collective-permute-done.13.refs_1_), channel_id=1, source_target_pairs={{0,1},{1,0},{2,3},{3,2},{4,5},{5,4},{6,7},{7,6},{8,9},{9,8},{10,11... | collective-permute-start | bytes 3145736 | tf_op jit(solution)/shard_map/ppermute | solution.py:25
  78.0 19.3 %collective-permute-start.19 = (bf16[1024,512]{1,0:T(8,128)(2,1)}, bf16[1024,512]{1,0:T(8,128)(2,1)}, u32[]{:S(2)}, u32[]{:S(2)}) collective-permute-start(bf16[1024,512]{1,0:T(8,128)(2,1)} %collective-permute-done.15.refs_2_), channel_id=1, source_target_pairs={{0,1},{1,0},{2,3},{3,2},{4,5},{5,4},{6,7},{7,6},{8,9},{9,8},{10,11... | collective-permute-start | bytes 3145736 | tf_op jit(solution)/shard_map/ppermute | solution.py:25
  88.8 8.5 %collective-permute-start.20 = (bf16[512,512]{1,0:T(8,128)(2,1)S(1)}, bf16[512,512]{1,0:T(8,128)(2,1)}, u32[]{:S(2)}, u32[]{:S(2)}) collective-permute-start(bf16[512,512]{1,0:T(8,128)(2,1)S(1)} %collective-permute-done.14.refs_3_), channel_id=1, source_target_pairs={{0,1},{1,0},{2,3},{3,2},{4,5},{5,4},{6,7},{7,6},{8,9},{9,8},{10,11... | collective-permute-start | bytes 1572872 | tf_op jit(solution)/shard_map/ppermute | solution.py:25
  93.5 22.4 %all-to-all-start.1 = ((bf16[8,16,1536]{2,1,0:T(8,128)(2,1)}), bf16[8,16,1536]{2,1,0:T(8,128)(2,1)S(1)}, u32[]{:S(2)}, u32[]{:S(2)}) async-start(bf16[8,16,1536]{2,1,0:T(8,128)(2,1)} %broadcast_in_dim.2), calls=%async_computation.1 | async-start | bytes 786432 | tf_op jit(solution)/shard_map/all_to_all | solution.py:313
  115.8 15.0 %collective-permute-start.22 = (bf16[128,1536]{1,0:T(8,128)(2,1)S(1)}, bf16[128,1536]{1,0:T(8,128)(2,1)S(1)}, u32[]{:S(2)}, u32[]{:S(2)}) collective-permute-start(bf16[128,1536]{1,0:T(8,128)(2,1)S(1)} %bitcast.81), channel_id=1, source_target_pairs={{0,64},{64,0},{128,192},{192,128},{1,65},{65,1},{129,193},{193,129... | collective-permute-start | bytes 1179656 | tf_op jit(solution)/shard_map/ppermute | solution.py:47
  115.9 15.0 %collective-permute-start.23 = (bf16[128,1536]{1,0:T(8,128)(2,1)S(1)}, bf16[128,1536]{1,0:T(8,128)(2,1)S(1)}, u32[]{:S(2)}, u32[]{:S(2)}) collective-permute-start(bf16[128,1536]{1,0:T(8,128)(2,1)S(1)} %bitcast.82), channel_id=1, source_target_pairs={{0,192},{64,128},{128,64},{192,0},{1,193},{65,129},{129,65},{193,1... | collective-permute-start | bytes 1179656 | tf_op jit(solution)/shard_map/ppermute | solution.py:43
  123.8 15.1 %collective-permute-start.7 = (bf16[8,256,128]{2,1,0:T(8,128)(2,1)S(1)}, bf16[8,256,128]{2,1,0:T(8,128)(2,1)S(1)}, u32[]{:S(2)}, u32[]{:S(2)}) collective-permute-start(bf16[8,256,128]{2,1,0:T(8,128)(2,1)S(1)} %slice_bitcast_fusion), channel_id=1, source_target_pairs={{0,64},{64,0},{128,192},{192,128},{1,65},{65,1},{129,193},{193,129... | collective-permute-start | bytes 1572872 | tf_op jit(solution)/shard_map/ppermute | solution.py:47
  130.9 17.6 %collective-permute-start.26 = (bf16[512,512]{1,0:T(8,128)(2,1)S(1)}, bf16[512,512]{1,0:T(8,128)(2,1)S(1)}, u32[]{:S(2)}, u32[]{:S(2)}) collective-permute-start(bf16[512,512]{1,0:T(8,128)(2,1)S(1)} %shard_map.95), channel_id=1, source_target_pairs={{0,192},{64,128},{128,64},{192,0},{1,193},{65,129},{129,65},{193,1... | collective-permute-start | bytes 1572872 | tf_op jit(solution)/shard_map/ppermute | solution.py:43
  132.8 15.7 %collective-permute-start.25 = (bf16[128,1536]{1,0:T(8,128)(2,1)S(1)}, bf16[128,1536]{1,0:T(8,128)(2,1)S(1)}, u32[]{:S(2)}, u32[]{:S(2)}) collective-permute-start(bf16[128,1536]{1,0:T(8,128)(2,1)S(1)} %collective-permute-done.23.refs_2_), channel_id=1, source_target_pairs={{0,64},{64,0},{128,192},{192,128},{1,65},{65,1},{129,193},{193,129... | collective-permute-start | bytes 1179656 | tf_op jit(solution)/shard_map/ppermute | solution.py:47
  142.9 7.8 %collective-permute-start.24 = (bf16[512,256]{1,0:T(8,128)(2,1)S(1)}, bf16[512,256]{1,0:T(8,128)(2,1)S(1)}, u32[]{:S(2)}, u32[]{:S(2)}) collective-permute-start(bf16[512,256]{1,0:T(8,128)(2,1)S(1)} %shard_map.97), channel_id=1, source_target_pairs={{0,192},{64,128},{128,64},{192,0},{1,193},{65,129},{129,65},{193,1... | collective-permute-start | bytes 786440 | tf_op jit(solution)/shard_map/ppermute | solution.py:43
  (11 other events, 146.4 us)
Sparse Core Ops, SparseCore 0:
  32.0 90.6 all-gather.2

commit v3 on v2

--- a/solution.py
+++ b/solution.py
@@ -117,14 +117,26 @@
     )(blocks, places, *mine, *other, projector)
 
 
-def product_kernel(part_ref, left_ref, one, two, three, four, out_ref, whole_ref):
+def product_kernel(features, part_ref, left_ref, one, two, three, four, out_ref, whole_ref, sum_ref):
     half, lanes = one.shape[-2:]
     for i, (first, second) in enumerate(((one, two), (three, four))):
         columns = pl.ds(i * lanes, lanes)
         whole_ref[:, :half, columns] = first[...].reshape(-1, half, lanes)
         whole_ref[:, half:, columns] = second[...].reshape(-1, half, lanes)
     whole = whole_ref[...].reshape(-1, 2 * lanes)
-    out_ref[...] = jnp.dot(left_ref[...], whole, preferred_element_type=f32).astype(out_ref.dtype)
+    value = jnp.dot(left_ref[...], whole, preferred_element_type=f32)
+
+    if whole.shape[0] == features:
+        out_ref[...] = value.astype(out_ref.dtype)
+        return
+
+    @pl.when(pl.program_id(1) == 0)
+    def _():
+        sum_ref[...] = value
+
+    @pl.when(pl.program_id(1) == 1)
+    def _():
+        out_ref[...] = (sum_ref[...] + value).astype(out_ref.dtype)
 
 
 def product(left, part, weight, first, tiles, dtype, beside=None):
@@ -132,24 +144,34 @@
     places, blocks, half, lanes = weight.shape
     pairs = blocks // 2 + 1
 
+    halves = 2 if tiles == 1 else 1
+
     def block(at):
-        return pl.BlockSpec((places, 1, half, lanes), lambda j, part: (0, at + 2 * j, 0, 0))
+        return pl.BlockSpec(
+            (places // halves, 1, half, lanes), lambda j, k, part: (k, at + 2 * j, 0, 0)
+        )
 
     specs = [block(first), block(first + pairs), block(first + 1), block(first + 1 + pairs)]
     arrays = [weight] * 4
     if beside is not None:
-        specs[3] = pl.BlockSpec(beside.shape, lambda j, part: (0, 0, 0))
+        specs[3] = pl.BlockSpec((places // halves, half, lanes), lambda j, k, part: (k, 0, 0))
         arrays[3] = beside
     columns = tiles * 2 * lanes
     return pl.pallas_call(
-        product_kernel,
+        functools.partial(product_kernel, features),
         out_shape=jax.ShapeDtypeStruct((rows, columns), dtype),
         grid_spec=pltpu.PrefetchScalarGridSpec(
             num_scalar_prefetch=1,
-            grid=(tiles,),
-            in_specs=[pl.BlockSpec((rows, features), lambda j, part: (part[0], 0)), *specs],
-            out_specs=pl.BlockSpec((rows, 2 * lanes), lambda j, part: (0, j)),
-            scratch_shapes=[pltpu.VMEM((places, 2 * half, 2 * lanes), bf16)],
+            grid=(tiles, halves),
+            in_specs=[
+                pl.BlockSpec((rows, features // halves), lambda j, k, part: (part[0], k)),
+                *specs,
+            ],
+            out_specs=pl.BlockSpec((rows, 2 * lanes), lambda j, k, part: (0, j)),
+            scratch_shapes=[
+                pltpu.VMEM((places // halves, 2 * half, 2 * lanes), bf16),
+                pltpu.VMEM((rows, 2 * lanes), f32),
+            ],
         ),
         compiler_params=pltpu.CompilerParams(vmem_limit_bytes=48 << 20),
         cost_estimate=pl.CostEstimate(

time: 160 us -> 159 us (level)
  transfers between devices with their start and end apart: 30 -> 30, of which waited for: 11 -> 12; matrix products, arithmetic and copies ran while one was open for 12% -> 12% of each run, Pallas kernels for 21% -> 20%
where the time goes in v3:
time: 159 us; the launch traced here: 158 us
  starting transfers between devices  50.5 us (32%)
  waiting for transfers between devices  38.9 us (24%)
  Pallas kernels  32.8 us (21%)
  between operations  14.5 us (9%)
  local copies, waits for them, and re-layouts  9.23 us (6%)
  matrix products  7.21 us (5%)
  other arithmetic  4.7 us (3%)
    ppermute x18, starting transfers between devices, shift(): lax.ppermute(block, axis, [(i, (i + by) % size) for i in range(size)])  26.3 us
    pallas_call x4, Pallas kernels, product(): pl.pallas_call(functools.partial(product_kernel, features), out_shape=jax...  18.5 us
    ppermute x18, waiting for transfers between devices, shift(): lax.ppermute(block, axis, [(i, (i + by) % size) for i in range(size)])  16.2 us
    pallas_call x1, Pallas kernels, prepare(): pl.pallas_call(prepare_kernel, out_shape=(jax.ShapeDtypeStruct((2 * rows,...  11.1 us
    ppermute x5, starting transfers between devices, facing(): return lax.ppermute(block, Y, [(i, 3 - i) for i in range(4)])  9.79 us
    all_to_all x1, starting transfers between devices, body(): low_grad = lax.all_to_all(summed, 'z', 0, 0)  8.52 us
    all_to_all x1, waiting for transfers between devices, body(): lax.all_to_all(jnp.broadcast_to(normed[None], (8, *normed.shape)), 'z', 0...  7.28 us
    ppermute x5, waiting for transfers between devices, facing(): return lax.ppermute(block, Y, [(i, 3 - i) for i in range(4)])  6.09 us
  transfers between devices with their start and end apart: 30, of which 12 were waited for; matrix products, arithmetic and copies ran while one was open for 12% of the time, Pallas kernels for 20%

profile of v3, /device:TPU:1, one launch (start us, length us, event | category | flops | bytes accessed | tf_op | source)
XLA Modules:
  0.0 157.8 jit_solution(1114130934048836186)
XLA Ops:
  7.2 2.1 %collective-permute-start = (bf16[256,512]{1,0:T(8,128)(2,1)}, bf16[256,512]{1,0:T(8,128)(2,1)S(1)}, u32[]{:S(2)}, u32[]{:S(2)}) collective-permute-start(bf16[256,512]{1,0:T(8,128)(2,1)} %param.7), channel_id=1, source_target_pairs={{0,2},{2,4},{4,6},{6,0},{1,3},{3,5},{5,7},{7,1},{8,10},{10,12},{12... | collective-permute-start | bytes 786440 | tf_op jit(solution)/shard_map/ppermute | solution.py:25
  12.0 2.9 %collective-permute-start.2 = (bf16[6,128,128]{1,2,0:T(8,128)(2,1)S(1)}, bf16[6,128,128]{1,2,0:T(8,128)(2,1)S(1)}, u32[]{:S(2)}, u32[]{:S(2)}) collective-permute-start(bf16[6,128,128]{1,2,0:T(8,128)(2,1)S(1)} %get-tuple-element.73), channel_id=1, source_target_pairs={{0,192},{64,128},{128,64},{192,0},{1,193},{65,129},{129,65},{193,1... | collective-permute-start | bytes 589832 | tf_op jit(solution)/shard_map/ppermute | solution.py:43
  20.5 2.5 %collective-permute-start.4 = (bf16[128,512]{1,0:T(8,128)(2,1)S(1)}, bf16[128,512]{1,0:T(8,128)(2,1)S(1)}, u32[]{:S(2)}, u32[]{:S(2)}) collective-permute-start(bf16[128,512]{1,0:T(8,128)(2,1)S(1)} %slice.63), channel_id=1, source_target_pairs={{0,6},{2,0},{4,2},{6,4},{1,7},{3,1},{5,3},{7,5},{8,14},{10,8},{12,... | collective-permute-start | bytes 393224 | tf_op jit(solution)/shard_map/ppermute | solution.py:25
  25.6 4.3 %collective-permute-done.5 = bf16[512,512]{1,0:T(8,128)(2,1)S(1)} collective-permute-done((bf16[512,512]{1,0:T(8,128)(2,1)}, bf16[512,512]{1,0:T(8,128)(2,1)S(1)}, u32[]{:S(2)}, u32[]{:S(2)}) %collective-permute-start.5) | collective-permute-done | bytes 524320 | tf_op jit(solution)/shard_map/ppermute | solution.py:43
  33.4 3.0 %collective-permute-start.8 = (f32[256,512]{0,1:T(8,128)S(1)}, f32[256,512]{0,1:T(8,128)}, u32[]{:S(2)}, u32[]{:S(2)}) collective-permute-start(f32[256,512]{0,1:T(8,128)S(1)} %add.300), channel_id=1, source_target_pairs={{0,1},{1,0},{2,3},{3,2},{4,5},{5,4},{6,7},{7,6},{8,9},{9,8},{10,11... | collective-permute-start | bytes 1572872 | tf_op jit(solution)/shard_map/ppermute | solution.py:25
  44.4 2.7 %collective-permute-start.15 = (bf16[1024,512]{1,0:T(8,128)(2,1)}, bf16[1024,512]{1,0:T(8,128)(2,1)}, u32[]{:S(2)}, u32[]{:S(2)}) collective-permute-start(bf16[1024,512]{1,0:T(8,128)(2,1)} %constant_dynamic-update-slice_fusion.refs_0_), channel_id=1, source_target_pairs={{0,6},{2,0},{4,2},{6,4},{1,7},{3,1},{5,3},{7,5},{8,14},{10,8},{12,... | collective-permute-start | bytes 3145736 | tf_op jit(solution)/shard_map/ppermute | solution.py:25
  50.4 2.7 %collective-permute-start.12 = (bf16[128,1536]{1,0:T(8,128)(2,1)}, bf16[128,1536]{1,0:T(8,128)(2,1)}, u32[]{:S(2)}, u32[]{:S(2)}) collective-permute-start(bf16[128,1536]{1,0:T(8,128)(2,1)} %pad_maximum_fusion.3), channel_id=1, source_target_pairs={{0,192},{64,0},{128,64},{192,128},{1,193},{65,1},{129,65},{193,129... | collective-permute-start | bytes 1179656 | tf_op jit(solution)/shard_map/ppermute | solution.py:25
  53.1 7.2 %collective-permute-done.11 = bf16[128,1536]{1,0:T(8,128)(2,1)} collective-permute-done((bf16[128,1536]{1,0:T(8,128)(2,1)}, bf16[128,1536]{1,0:T(8,128)(2,1)}, u32[]{:S(2)}, u32[]{:S(2)}) %collective-permute-start.11) | collective-permute-done | bytes 393248 | tf_op jit(solution)/shard_map/ppermute | solution.py:25
  62.3 8.5 %all-to-all-start = ((bf16[8,16,1536]{2,1,0:T(8,128)(2,1)}), bf16[8,16,1536]{2,1,0:T(8,128)(2,1)S(1)}, u32[]{:S(2)}, u32[]{:S(2)}) async-start(bf16[8,16,1536]{2,1,0:T(8,128)(2,1)} %bitcast.104), calls=%async_computation | async-start | bytes 786432 | tf_op jit(solution)/shard_map/all_to_all | solution.py:325
  72.0 2.7 %collective-permute-start.16 = (bf16[512,512]{1,0:T(8,128)(2,1)S(1)}, bf16[512,512]{1,0:T(8,128)(2,1)S(1)}, u32[]{:S(2)}, u32[]{:S(2)}) collective-permute-start(bf16[512,512]{1,0:T(8,128)(2,1)S(1)} %slice.86), channel_id=1, source_target_pairs={{0,6},{2,0},{4,2},{6,4},{1,7},{3,1},{5,3},{7,5},{8,14},{10,8},{12,... | collective-permute-start | bytes 1572872 | tf_op jit(solution)/shard_map/ppermute | solution.py:25
  74.8 3.2 %collective-permute-start.17 = (bf16[1024,512]{1,0:T(8,128)(2,1)}, bf16[1024,512]{1,0:T(8,128)(2,1)}, u32[]{:S(2)}, u32[]{:S(2)}) collective-permute-start(bf16[1024,512]{1,0:T(8,128)(2,1)} %constant_dynamic-update-slice_fusion.refs_0_), channel_id=1, source_target_pairs={{0,1},{1,0},{2,3},{3,2},{4,5},{5,4},{6,7},{7,6},{8,9},{9,8},{10,11... | collective-permute-start | bytes 3145736 | tf_op jit(solution)/shard_map/ppermute | solution.py:25
  78.5 4.5 %collective-permute-done.14.refs_3_ = bf16[512,512]{1,0:T(8,128)(2,1)S(1)} collective-permute-done((bf16[512,512]{1,0:T(8,128)(2,1)S(1)}, bf16[512,512]{1,0:T(8,128)(2,1)S(1)}, u32[]{:S(2)}, u32[]{:S(2)}) %collective-permute-start.14) | collective-permute-done | bytes 524320 | tf_op jit(solution)/shard_map/ppermute | solution.py:25
  83.0 5.7 %all-to-all-done = bf16[8,16,1536]{2,1,0:T(8,128)(2,1)S(1)} async-done(((bf16[8,16,1536]{2,1,0:T(8,128)(2,1)}), bf16[8,16,1536]{2,1,0:T(8,128)(2,1)S(1)}, u32[]{:S(2)}, u32[]{:S(2)}) %all-to-all-start) | async-done | bytes 393248 | tf_op jit(solution)/shard_map/all_to_all | solution.py:325
  88.8 3.2 %collective-permute-start.20 = (bf16[512,512]{1,0:T(8,128)(2,1)S(1)}, bf16[512,512]{1,0:T(8,128)(2,1)}, u32[]{:S(2)}, u32[]{:S(2)}) collective-permute-start(bf16[512,512]{1,0:T(8,128)(2,1)S(1)} %collective-permute-done.14.refs_3_), channel_id=1, source_target_pairs={{0,1},{1,0},{2,3},{3,2},{4,5},{5,4},{6,7},{7,6},{8,9},{9,8},{10,11... | collective-permute-start | bytes 1572872 | tf_op jit(solution)/shard_map/ppermute | solution.py:25
  93.5 3.5 %all-to-all-start.1 = ((bf16[8,16,1536]{2,1,0:T(8,128)(2,1)}), bf16[8,16,1536]{2,1,0:T(8,128)(2,1)S(1)}, u32[]{:S(2)}, u32[]{:S(2)}) async-start(bf16[8,16,1536]{2,1,0:T(8,128)(2,1)} %broadcast_in_dim.2), calls=%async_computation.1 | async-start | bytes 786432 | tf_op jit(solution)/shard_map/all_to_all | solution.py:335
  97.3 11.1 %shard_map.94 = (bf16[1024,4096]{1,0:T(8,128)(2,1)}, bf16[512,512]{1,0:T(8,128)(2,1)S(1)}) custom-call(s32[8]{0:T(128)S(1)} %stack.134.blocks_ref, s32[32]{0:T(128)S(1)} %stack.167.places_ref, bf16[1024,512]{1,0:T(8,128)(2,1)} %constant_dynamic-update-slice_fusion.refs_0_, bf16[1024,512]{1,0:T(8,128)(2,1)S(1)} %collective-permute-done.13.refs_1_, ...), custom_call_target="tpu_custom_call" | custom-call | flops 2147483648 | bytes 20971520 | tf_op jit(solution)/shard_map/pallas_call | solution.py:94
  108.6 7.3 %all-to-all-done.1 = bf16[8,16,1536]{2,1,0:T(8,128)(2,1)S(1)} async-done(((bf16[8,16,1536]{2,1,0:T(8,128)(2,1)}), bf16[8,16,1536]{2,1,0:T(8,128)(2,1)S(1)}, u32[]{:S(2)}, u32[]{:S(2)}) %all-to-all-start.1) | async-done | bytes 393248 | tf_op jit(solution)/shard_map/all_to_all | solution.py:335
  115.9 3.3 %collective-permute-start.23 = (bf16[128,1536]{1,0:T(8,128)(2,1)S(1)}, bf16[128,1536]{1,0:T(8,128)(2,1)S(1)}, u32[]{:S(2)}, u32[]{:S(2)}) collective-permute-start(bf16[128,1536]{1,0:T(8,128)(2,1)S(1)} %bitcast.82), channel_id=1, source_target_pairs={{0,192},{64,128},{128,64},{192,0},{1,193},{65,129},{129,65},{193,1... | collective-permute-start | bytes 1179656 | tf_op jit(solution)/shard_map/ppermute | solution.py:43
  119.2 3.5 %all-gather.3.cloned.1.call-done = bf16[88,256,128]{2,1,0:T(8,128)(2,1)} async-done(((bf16[11,256,128]{2,1,0:T(8,128)(2,1)}), bf16[88,256,128]{2,1,0:T(8,128)(2,1)}) %all-gather.3.cloned.1.call-update) | async-done | bytes 5767184 | tf_op jit(solution)/shard_map/all_gather | solution.py:302
  125.1 5.7 %shard_map.95 = bf16[512,512]{1,0:T(8,128)(2,1)S(1)} custom-call(s32[1]{0:T(128)} %constant.92.clone.1.part_ref, bf16[1024,4096]{1,0:T(8,128)(2,1)} %get-tuple-element.57.left_ref, bf16[8,11,256,128]{3,2,1,0:T(8,128)(2,1)} %bitcast.86, bf16[8,11,256,128]{3,2,1,0:T(8,128)(2,1)} %bitcast.87, bf16[8,11,256,128]{3,2,1,0:T(8,128)(2,1)} %bitcast.88, ...), custom_call_target="tpu_custom_call" | custom-call | flops 2147483648 | bytes 9437184 | tf_op jit(solution)/shard_map/pallas_call | solution.py:160
  133.1 5.8 %shard_map.96.own_one = f32[512,512]{1,0:T(8,128)S(1)} custom-call(s32[1]{0:T(128)} %constant.100.clone.1.part_ref, bf16[1024,4096]{1,0:T(8,128)(2,1)} %get-tuple-element.57.left_ref, bf16[8,11,256,128]{3,2,1,0:T(8,128)(2,1)} %bitcast.90, bf16[8,11,256,128]{3,2,1,0:T(8,128)(2,1)} %bitcast.91, bf16[8,11,256,128]{3,2,1,0:T(8,128)(2,1)} %bitcast.92, ...), custom_call_target="tpu_custom_call" | custom-call | flops 2147483648 | bytes 9437184 | tf_op jit(solution)/shard_map/pallas_call | solution.py:160
  138.9 3.5 %shard_map.97 = bf16[512,256]{1,0:T(8,128)(2,1)S(1)} custom-call(s32[1]{0:T(128)} %constant.92.clone.1.part_ref, bf16[1024,4096]{1,0:T(8,128)(2,1)} %get-tuple-element.57.left_ref, bf16[8,11,256,128]{3,2,1,0:T(8,128)(2,1)} %bitcast.94, bf16[8,11,256,128]{3,2,1,0:T(8,128)(2,1)} %bitcast.95, bf16[8,11,256,128]{3,2,1,0:T(8,128)(2,1)} %bitcast.96, ...), custom_call_target="tpu_custom_call" | custom-call | flops 1073741824 | bytes 6815744 | tf_op jit(solution)/shard_map/pallas_call | solution.py:160
  143.9 3.5 %shard_map.98.own_two = f32[512,256]{1,0:T(8,128)S(1)} custom-call(s32[1]{0:T(128)} %constant.100.clone.1.part_ref, bf16[1024,4096]{1,0:T(8,128)(2,1)} %get-tuple-element.57.left_ref, bf16[8,11,256,128]{3,2,1,0:T(8,128)(2,1)} %bitcast.97, bf16[8,11,256,128]{3,2,1,0:T(8,128)(2,1)} %bitcast.98, bf16[8,11,256,128]{3,2,1,0:T(8,128)(2,1)} %bitcast.99, ...), custom_call_target="tpu_custom_call" | custom-call | flops 1073741824 | bytes 6815744 | tf_op jit(solution)/shard_map/pallas_call | solution.py:160
  147.4 2.2 %shard_map.99.refs_4_ = bf16[512,1536]{1,0:T(8,128)(2,1)} custom-call(s32[1]{0:T(128)} %bitcast.group_ref, f32[512,512]{1,0:T(8,128)S(1)} %shard_map.96.own_one, f32[512,256]{1,0:T(8,128)S(1)} %shard_map.98.own_two, bf16[512,512]{1,0:T(8,128)(2,1)S(1)} %collective-permute-done.26.sent_one, bf16[512,512]{1,0:T(8,128)(2,1)S(1)} %pad_maximum_fusion.1.low_ref, ...), custom_call_target="tpu_custom_call" | custom-call | flops 671088640 | bytes 4587520 | tf_op jit(solution)/shard_map/pallas_call | solution.py:220
  (84 shorter events, 38.8 us)
Async XLA Ops:
  7.2 115.5 %all-gather.3.cloned.1.call-start = ((), (), s32[]{:S(2)}) async-start(), calls=%async_computation.2 | async-start | bytes 6488064 | tf_op jit(solution)/shard_map/all_gather | solution.py:302
  7.2 10.7 %collective-permute-start = (bf16[256,512]{1,0:T(8,128)(2,1)}, bf16[256,512]{1,0:T(8,128)(2,1)S(1)}, u32[]{:S(2)}, u32[]{:S(2)}) collective-permute-start(bf16[256,512]{1,0:T(8,128)(2,1)} %param.7), channel_id=1, source_target_pairs={{0,2},{2,4},{4,6},{6,0},{1,3},{3,5},{5,7},{7,1},{8,10},{10,12},{12... | collective-permute-start | bytes 786440 | tf_op jit(solution)/shard_map/ppermute | solution.py:25
  9.3 8.6 %collective-permute-start.1 = (bf16[256,512]{1,0:T(8,128)(2,1)}, bf16[256,512]{1,0:T(8,128)(2,1)S(1)}, u32[]{:S(2)}, u32[]{:S(2)}) collective-permute-start(bf16[256,512]{1,0:T(8,128)(2,1)} %param.7), channel_id=1, source_target_pairs={{0,6},{2,0},{4,2},{6,4},{1,7},{3,1},{5,3},{7,5},{8,14},{10,8},{12,... | collective-permute-start | bytes 786440 | tf_op jit(solution)/shard_map/ppermute | solution.py:25
  14.9 15.0 %collective-permute-start.5 = (bf16[512,512]{1,0:T(8,128)(2,1)}, bf16[512,512]{1,0:T(8,128)(2,1)S(1)}, u32[]{:S(2)}, u32[]{:S(2)}) collective-permute-start(bf16[512,512]{1,0:T(8,128)(2,1)} %param.13), channel_id=1, source_target_pairs={{0,192},{64,128},{128,64},{192,0},{1,193},{65,129},{129,65},{193,1... | collective-permute-start | bytes 1572872 | tf_op jit(solution)/shard_map/ppermute | solution.py:43
  18.0 12.6 %collective-permute-start.6 = (bf16[5,256,128]{1,2,0:T(8,128)(2,1)S(1)}, bf16[5,256,128]{1,2,0:T(8,128)(2,1)S(1)}, u32[]{:S(2)}, u32[]{:S(2)}) collective-permute-start(bf16[5,256,128]{1,2,0:T(8,128)(2,1)S(1)} %pad_maximum_fusion.4), channel_id=1, source_target_pairs={{0,64},{64,0},{128,192},{192,128},{1,65},{65,1},{129,193},{193,129... | collective-permute-start | bytes 983048 | tf_op jit(solution)/shard_map/ppermute | solution.py:47
  39.8 7.4 %collective-permute-start.10 = (bf16[64,1536]{1,0:T(8,128)(2,1)S(1)}, bf16[64,1536]{1,0:T(8,128)(2,1)S(1)}, u32[]{:S(2)}, u32[]{:S(2)}) collective-permute-start(bf16[64,1536]{1,0:T(8,128)(2,1)S(1)} %get-tuple-element.67), channel_id=1, source_target_pairs={{0,192},{64,0},{128,64},{192,128},{1,193},{65,1},{129,65},{193,129... | collective-permute-start | bytes 589832 | tf_op jit(solution)/shard_map/ppermute | solution.py:25
  44.4 26.4 %collective-permute-start.13 = (bf16[1024,512]{1,0:T(8,128)(2,1)}, bf16[1024,512]{1,0:T(8,128)(2,1)S(1)}, u32[]{:S(2)}, u32[]{:S(2)}) collective-permute-start(bf16[1024,512]{1,0:T(8,128)(2,1)} %constant_dynamic-update-slice_fusion.refs_0_), channel_id=1, source_target_pairs={{0,2},{2,4},{4,6},{6,0},{1,3},{3,5},{5,7},{7,1},{8,10},{10,12},{12... | collective-permute-start | bytes 3145736 | tf_op jit(solution)/shard_map/ppermute | solution.py:25
  44.4 26.5 %collective-permute-start.15 = (bf16[1024,512]{1,0:T(8,128)(2,1)}, bf16[1024,512]{1,0:T(8,128)(2,1)}, u32[]{:S(2)}, u32[]{:S(2)}) collective-permute-start(bf16[1024,512]{1,0:T(8,128)(2,1)} %constant_dynamic-update-slice_fusion.refs_0_), channel_id=1, source_target_pairs={{0,6},{2,0},{4,2},{6,4},{1,7},{3,1},{5,3},{7,5},{8,14},{10,8},{12,... | collective-permute-start | bytes 3145736 | tf_op jit(solution)/shard_map/ppermute | solution.py:25
  49.6 10.6 %collective-permute-start.11 = (bf16[128,1536]{1,0:T(8,128)(2,1)}, bf16[128,1536]{1,0:T(8,128)(2,1)}, u32[]{:S(2)}, u32[]{:S(2)}) collective-permute-start(bf16[128,1536]{1,0:T(8,128)(2,1)} %pad_maximum_fusion.2), channel_id=1, source_target_pairs={{0,64},{64,128},{128,192},{192,0},{1,65},{65,129},{129,193},{193,1... | collective-permute-start | bytes 1179656 | tf_op jit(solution)/shard_map/ppermute | solution.py:25
  50.4 9.8 %collective-permute-start.12 = (bf16[128,1536]{1,0:T(8,128)(2,1)}, bf16[128,1536]{1,0:T(8,128)(2,1)}, u32[]{:S(2)}, u32[]{:S(2)}) collective-permute-start(bf16[128,1536]{1,0:T(8,128)(2,1)} %pad_maximum_fusion.3), channel_id=1, source_target_pairs={{0,192},{64,0},{128,64},{192,128},{1,193},{65,1},{129,65},{193,129... | collective-permute-start | bytes 1179656 | tf_op jit(solution)/shard_map/ppermute | solution.py:25
  62.3 26.5 %all-to-all-start = ((bf16[8,16,1536]{2,1,0:T(8,128)(2,1)}), bf16[8,16,1536]{2,1,0:T(8,128)(2,1)S(1)}, u32[]{:S(2)}, u32[]{:S(2)}) async-start(bf16[8,16,1536]{2,1,0:T(8,128)(2,1)} %bitcast.104), calls=%async_computation | async-start | bytes 786432 | tf_op jit(solution)/shard_map/all_to_all | solution.py:325
  70.8 12.1 %collective-permute-start.14 = (bf16[512,512]{1,0:T(8,128)(2,1)S(1)}, bf16[512,512]{1,0:T(8,128)(2,1)S(1)}, u32[]{:S(2)}, u32[]{:S(2)}) collective-permute-start(bf16[512,512]{1,0:T(8,128)(2,1)S(1)} %slice.85), channel_id=1, source_target_pairs={{0,2},{2,4},{4,6},{6,0},{1,3},{3,5},{5,7},{7,1},{8,10},{10,12},{12... | collective-permute-start | bytes 1572872 | tf_op jit(solution)/shard_map/ppermute | solution.py:25
  72.0 11.0 %collective-permute-start.16 = (bf16[512,512]{1,0:T(8,128)(2,1)S(1)}, bf16[512,512]{1,0:T(8,128)(2,1)S(1)}, u32[]{:S(2)}, u32[]{:S(2)}) collective-permute-start(bf16[512,512]{1,0:T(8,128)(2,1)S(1)} %slice.86), channel_id=1, source_target_pairs={{0,6},{2,0},{4,2},{6,4},{1,7},{3,1},{5,3},{7,5},{8,14},{10,8},{12,... | collective-permute-start | bytes 1572872 | tf_op jit(solution)/shard_map/ppermute | solution.py:25
  74.8 22.5 %collective-permute-start.17 = (bf16[1024,512]{1,0:T(8,128)(2,1)}, bf16[1024,512]{1,0:T(8,128)(2,1)}, u32[]{:S(2)}, u32[]{:S(2)}) collective-permute-start(bf16[1024,512]{1,0:T(8,128)(2,1)} %constant_dynamic-update-slice_fusion.refs_0_), channel_id=1, source_target_pairs={{0,1},{1,0},{2,3},{3,2},{4,5},{5,4},{6,7},{7,6},{8,9},{9,8},{10,11... | collective-permute-start | bytes 3145736 | tf_op jit(solution)/shard_map/ppermute | solution.py:25
  78.0 19.3 %collective-permute-start.18 = (bf16[1024,512]{1,0:T(8,128)(2,1)S(1)}, bf16[1024,512]{1,0:T(8,128)(2,1)}, u32[]{:S(2)}, u32[]{:S(2)}) collective-permute-start(bf16[1024,512]{1,0:T(8,128)(2,1)S(1)} %collective-permute-done.13.refs_1_), channel_id=1, source_target_pairs={{0,1},{1,0},{2,3},{3,2},{4,5},{5,4},{6,7},{7,6},{8,9},{9,8},{10,11... | collective-permute-start | bytes 3145736 | tf_op jit(solution)/shard_map/ppermute | solution.py:25
  78.0 19.3 %collective-permute-start.19 = (bf16[1024,512]{1,0:T(8,128)(2,1)}, bf16[1024,512]{1,0:T(8,128)(2,1)}, u32[]{:S(2)}, u32[]{:S(2)}) collective-permute-start(bf16[1024,512]{1,0:T(8,128)(2,1)} %collective-permute-done.15.refs_2_), channel_id=1, source_target_pairs={{0,1},{1,0},{2,3},{3,2},{4,5},{5,4},{6,7},{7,6},{8,9},{9,8},{10,11... | collective-permute-start | bytes 3145736 | tf_op jit(solution)/shard_map/ppermute | solution.py:25
  88.8 8.5 %collective-permute-start.20 = (bf16[512,512]{1,0:T(8,128)(2,1)S(1)}, bf16[512,512]{1,0:T(8,128)(2,1)}, u32[]{:S(2)}, u32[]{:S(2)}) collective-permute-start(bf16[512,512]{1,0:T(8,128)(2,1)S(1)} %collective-permute-done.14.refs_3_), channel_id=1, source_target_pairs={{0,1},{1,0},{2,3},{3,2},{4,5},{5,4},{6,7},{7,6},{8,9},{9,8},{10,11... | collective-permute-start | bytes 1572872 | tf_op jit(solution)/shard_map/ppermute | solution.py:25
  93.5 22.4 %all-to-all-start.1 = ((bf16[8,16,1536]{2,1,0:T(8,128)(2,1)}), bf16[8,16,1536]{2,1,0:T(8,128)(2,1)S(1)}, u32[]{:S(2)}, u32[]{:S(2)}) async-start(bf16[8,16,1536]{2,1,0:T(8,128)(2,1)} %broadcast_in_dim.2), calls=%async_computation.1 | async-start | bytes 786432 | tf_op jit(solution)/shard_map/all_to_all | solution.py:335
  115.8 15.0 %collective-permute-start.22 = (bf16[128,1536]{1,0:T(8,128)(2,1)S(1)}, bf16[128,1536]{1,0:T(8,128)(2,1)S(1)}, u32[]{:S(2)}, u32[]{:S(2)}) collective-permute-start(bf16[128,1536]{1,0:T(8,128)(2,1)S(1)} %bitcast.81), channel_id=1, source_target_pairs={{0,64},{64,0},{128,192},{192,128},{1,65},{65,1},{129,193},{193,129... | collective-permute-start | bytes 1179656 | tf_op jit(solution)/shard_map/ppermute | solution.py:47
  115.9 15.0 %collective-permute-start.23 = (bf16[128,1536]{1,0:T(8,128)(2,1)S(1)}, bf16[128,1536]{1,0:T(8,128)(2,1)S(1)}, u32[]{:S(2)}, u32[]{:S(2)}) collective-permute-start(bf16[128,1536]{1,0:T(8,128)(2,1)S(1)} %bitcast.82), channel_id=1, source_target_pairs={{0,192},{64,128},{128,64},{192,0},{1,193},{65,129},{129,65},{193,1... | collective-permute-start | bytes 1179656 | tf_op jit(solution)/shard_map/ppermute | solution.py:43
  123.8 15.1 %collective-permute-start.7 = (bf16[8,256,128]{2,1,0:T(8,128)(2,1)S(1)}, bf16[8,256,128]{2,1,0:T(8,128)(2,1)S(1)}, u32[]{:S(2)}, u32[]{:S(2)}) collective-permute-start(bf16[8,256,128]{2,1,0:T(8,128)(2,1)S(1)} %slice_bitcast_fusion), channel_id=1, source_target_pairs={{0,64},{64,0},{128,192},{192,128},{1,65},{65,1},{129,193},{193,129... | collective-permute-start | bytes 1572872 | tf_op jit(solution)/shard_map/ppermute | solution.py:47
  130.9 16.5 %collective-permute-start.26 = (bf16[512,512]{1,0:T(8,128)(2,1)S(1)}, bf16[512,512]{1,0:T(8,128)(2,1)S(1)}, u32[]{:S(2)}, u32[]{:S(2)}) collective-permute-start(bf16[512,512]{1,0:T(8,128)(2,1)S(1)} %shard_map.95), channel_id=1, source_target_pairs={{0,192},{64,128},{128,64},{192,0},{1,193},{65,129},{129,65},{193,1... | collective-permute-start | bytes 1572872 | tf_op jit(solution)/shard_map/ppermute | solution.py:43
  132.8 14.6 %collective-permute-start.25 = (bf16[128,1536]{1,0:T(8,128)(2,1)S(1)}, bf16[128,1536]{1,0:T(8,128)(2,1)S(1)}, u32[]{:S(2)}, u32[]{:S(2)}) collective-permute-start(bf16[128,1536]{1,0:T(8,128)(2,1)S(1)} %collective-permute-done.23.refs_2_), channel_id=1, source_target_pairs={{0,64},{64,0},{128,192},{192,128},{1,65},{65,1},{129,193},{193,129... | collective-permute-start | bytes 1179656 | tf_op jit(solution)/shard_map/ppermute | solution.py:47
  142.4 7.6 %collective-permute-start.24 = (bf16[512,256]{1,0:T(8,128)(2,1)S(1)}, bf16[512,256]{1,0:T(8,128)(2,1)S(1)}, u32[]{:S(2)}, u32[]{:S(2)}) collective-permute-start(bf16[512,256]{1,0:T(8,128)(2,1)S(1)} %shard_map.97), channel_id=1, source_target_pairs={{0,192},{64,128},{128,64},{192,0},{1,193},{65,129},{129,65},{193,1... | collective-permute-start | bytes 786440 | tf_op jit(solution)/shard_map/ppermute | solution.py:43
  (11 other events, 146.4 us)
Sparse Core Ops, SparseCore 0:
  32.0 90.6 all-gather.2

commit v4 on v3

--- a/solution.py
+++ b/solution.py
@@ -117,24 +117,21 @@
     )(blocks, places, *mine, *other, projector)
 
 
-def product_kernel(features, part_ref, left_ref, one, two, three, four, out_ref, whole_ref, sum_ref):
-    half, lanes = one.shape[-2:]
-    for i, (first, second) in enumerate(((one, two), (three, four))):
+def product_kernel(part_ref, left_ref, *refs):
+    blocks, (out_ref, whole_ref, sum_ref) = refs[:-3], refs[-3:]
+    half, lanes = blocks[0].shape[-2:]
+    for i in range(len(blocks) // 2):
         columns = pl.ds(i * lanes, lanes)
-        whole_ref[:, :half, columns] = first[...].reshape(-1, half, lanes)
-        whole_ref[:, half:, columns] = second[...].reshape(-1, half, lanes)
-    whole = whole_ref[...].reshape(-1, 2 * lanes)
+        whole_ref[:, :half, columns] = blocks[2 * i][...].reshape(-1, half, lanes)
+        whole_ref[:, half:, columns] = blocks[2 * i + 1][...].reshape(-1, half, lanes)
+    whole = whole_ref[...].reshape(-1, whole_ref.shape[2])
     value = jnp.dot(left_ref[...], whole, preferred_element_type=f32)
 
-    if whole.shape[0] == features:
-        out_ref[...] = value.astype(out_ref.dtype)
-        return
-
-    @pl.when(pl.program_id(1) == 0)
+    @pl.when(pl.program_id(0) == 0)
     def _():
         sum_ref[...] = value
 
-    @pl.when(pl.program_id(1) == 1)
+    @pl.when(pl.program_id(0) == 1)
     def _():
         out_ref[...] = (sum_ref[...] + value).astype(out_ref.dtype)
 
@@ -143,34 +140,30 @@
     rows, features = left.shape[0] // 2, left.shape[1]
     places, blocks, half, lanes = weight.shape
     pairs = blocks // 2 + 1
-
-    halves = 2 if tiles == 1 else 1
-
-    def block(at):
-        return pl.BlockSpec(
-            (places // halves, 1, half, lanes), lambda j, k, part: (k, at + 2 * j, 0, 0)
-        )
-
-    specs = [block(first), block(first + pairs), block(first + 1), block(first + 1 + pairs)]
-    arrays = [weight] * 4
+    specs = [
+        pl.BlockSpec((places // 2, 1, half, lanes), lambda k, part, at=at: (k, at, 0, 0))
+        for i in range(2 * tiles)
+        for at in (first + i, min(first + i + pairs, blocks - 1))
+    ]
+    arrays = [weight] * len(specs)
     if beside is not None:
-        specs[3] = pl.BlockSpec((places // halves, half, lanes), lambda j, k, part: (k, 0, 0))
-        arrays[3] = beside
+        specs[-1] = pl.BlockSpec((places // 2, half, lanes), lambda k, part: (k, 0, 0))
+        arrays[-1] = beside
     columns = tiles * 2 * lanes
     return pl.pallas_call(
-        functools.partial(product_kernel, features),
+        product_kernel,
         out_shape=jax.ShapeDtypeStruct((rows, columns), dtype),
         grid_spec=pltpu.PrefetchScalarGridSpec(
             num_scalar_prefetch=1,
-            grid=(tiles, halves),
+            grid=(2,),
             in_specs=[
-                pl.BlockSpec((rows, features // halves), lambda j, k, part: (part[0], k)),
+                pl.BlockSpec((rows, features // 2), lambda k, part: (part[0], k)),
                 *specs,
             ],
-            out_specs=pl.BlockSpec((rows, 2 * lanes), lambda j, k, part: (0, j)),
+            out_specs=pl.BlockSpec((rows, columns), lambda k, part: (0, 0)),
             scratch_shapes=[
-                pltpu.VMEM((places // halves, 2 * half, 2 * lanes), bf16),
-                pltpu.VMEM((rows, 2 * lanes), f32),
+                pltpu.VMEM((places // 2, 2 * half, columns), bf16),
+                pltpu.VMEM((rows, columns), f32),
             ],
         ),
         compiler_params=pltpu.CompilerParams(vmem_limit_bytes=48 << 20),

time: 159 us -> 159 us (level)
  transfers between devices with their start and end apart: 30 -> 30, of which waited for: 12 -> 11; matrix products, arithmetic and copies ran while one was open for 12% -> 12% of each run, Pallas kernels for 20% -> 19%
where the time goes in v4:
time: 159 us; the launch traced here: 157 us
  starting transfers between devices  51.7 us (33%)
  waiting for transfers between devices  38.6 us (24%)
  Pallas kernels  31.6 us (20%)
  between operations  14.5 us (9%)
  local copies, waits for them, and re-layouts  9.23 us (6%)
  matrix products  7.21 us (5%)
  other arithmetic  4.7 us (3%)
    ppermute x18, starting transfers between devices, shift(): lax.ppermute(block, axis, [(i, (i + by) % size) for i in range(size)])  26.3 us
    pallas_call x4, Pallas kernels, product(): pl.pallas_call(product_kernel, out_shape=jax.ShapeDtypeStruct((rows, colu...  17.3 us
    ppermute x18, waiting for transfers between devices, shift(): lax.ppermute(block, axis, [(i, (i + by) % size) for i in range(size)])  16.2 us
    pallas_call x1, Pallas kernels, prepare(): pl.pallas_call(prepare_kernel, out_shape=(jax.ShapeDtypeStruct((2 * rows,...  11.1 us
    ppermute x5, starting transfers between devices, facing(): return lax.ppermute(block, Y, [(i, 3 - i) for i in range(4)])  11 us
    all_to_all x1, starting transfers between devices, body(): low_grad = lax.all_to_all(summed, 'z', 0, 0)  8.52 us
    all_to_all x1, waiting for transfers between devices, body(): lax.all_to_all(jnp.broadcast_to(normed[None], (8, *normed.shape)), 'z', 0...  7.28 us
    ppermute x5, waiting for transfers between devices, facing(): return lax.ppermute(block, Y, [(i, 3 - i) for i in range(4)])  5.79 us
  transfers between devices with their start and end apart: 30, of which 11 were waited for; matrix products, arithmetic and copies ran while one was open for 12% of the time, Pallas kernels for 19%

profile of v4, /device:TPU:1, one launch (start us, length us, event | category | flops | bytes accessed | tf_op | source)
XLA Modules:
  0.0 157.5 jit_solution(15914047007376511671)
XLA Ops:
  12.0 2.9 %collective-permute-start.2 = (bf16[6,128,128]{1,2,0:T(8,128)(2,1)S(1)}, bf16[6,128,128]{1,2,0:T(8,128)(2,1)S(1)}, u32[]{:S(2)}, u32[]{:S(2)}) collective-permute-start(bf16[6,128,128]{1,2,0:T(8,128)(2,1)S(1)} %get-tuple-element.73), channel_id=1, source_target_pairs={{0,192},{64,128},{128,64},{192,0},{1,193},{65,129},{129,65},{193,1... | collective-permute-start | bytes 589832 | tf_op jit(solution)/shard_map/ppermute | solution.py:43
  20.5 2.5 %collective-permute-start.4 = (bf16[128,512]{1,0:T(8,128)(2,1)S(1)}, bf16[128,512]{1,0:T(8,128)(2,1)S(1)}, u32[]{:S(2)}, u32[]{:S(2)}) collective-permute-start(bf16[128,512]{1,0:T(8,128)(2,1)S(1)} %slice.63), channel_id=1, source_target_pairs={{0,6},{2,0},{4,2},{6,4},{1,7},{3,1},{5,3},{7,5},{8,14},{10,8},{12,... | collective-permute-start | bytes 393224 | tf_op jit(solution)/shard_map/ppermute | solution.py:25
  25.6 4.3 %collective-permute-done.5 = bf16[512,512]{1,0:T(8,128)(2,1)S(1)} collective-permute-done((bf16[512,512]{1,0:T(8,128)(2,1)}, bf16[512,512]{1,0:T(8,128)(2,1)S(1)}, u32[]{:S(2)}, u32[]{:S(2)}) %collective-permute-start.5) | collective-permute-done | bytes 524320 | tf_op jit(solution)/shard_map/ppermute | solution.py:43
  33.4 3.0 %collective-permute-start.8 = (f32[256,512]{0,1:T(8,128)S(1)}, f32[256,512]{0,1:T(8,128)}, u32[]{:S(2)}, u32[]{:S(2)}) collective-permute-start(f32[256,512]{0,1:T(8,128)S(1)} %add.300), channel_id=1, source_target_pairs={{0,1},{1,0},{2,3},{3,2},{4,5},{5,4},{6,7},{7,6},{8,9},{9,8},{10,11... | collective-permute-start | bytes 1572872 | tf_op jit(solution)/shard_map/ppermute | solution.py:25
  44.4 2.7 %collective-permute-start.15 = (bf16[1024,512]{1,0:T(8,128)(2,1)}, bf16[1024,512]{1,0:T(8,128)(2,1)}, u32[]{:S(2)}, u32[]{:S(2)}) collective-permute-start(bf16[1024,512]{1,0:T(8,128)(2,1)} %constant_dynamic-update-slice_fusion.refs_0_), channel_id=1, source_target_pairs={{0,6},{2,0},{4,2},{6,4},{1,7},{3,1},{5,3},{7,5},{8,14},{10,8},{12,... | collective-permute-start | bytes 3145736 | tf_op jit(solution)/shard_map/ppermute | solution.py:25
  50.4 2.7 %collective-permute-start.12 = (bf16[128,1536]{1,0:T(8,128)(2,1)}, bf16[128,1536]{1,0:T(8,128)(2,1)}, u32[]{:S(2)}, u32[]{:S(2)}) collective-permute-start(bf16[128,1536]{1,0:T(8,128)(2,1)} %pad_maximum_fusion.3), channel_id=1, source_target_pairs={{0,192},{64,0},{128,64},{192,128},{1,193},{65,1},{129,65},{193,129... | collective-permute-start | bytes 1179656 | tf_op jit(solution)/shard_map/ppermute | solution.py:25
  53.1 7.2 %collective-permute-done.11 = bf16[128,1536]{1,0:T(8,128)(2,1)} collective-permute-done((bf16[128,1536]{1,0:T(8,128)(2,1)}, bf16[128,1536]{1,0:T(8,128)(2,1)}, u32[]{:S(2)}, u32[]{:S(2)}) %collective-permute-start.11) | collective-permute-done | bytes 393248 | tf_op jit(solution)/shard_map/ppermute | solution.py:25
  62.3 8.5 %all-to-all-start = ((bf16[8,16,1536]{2,1,0:T(8,128)(2,1)}), bf16[8,16,1536]{2,1,0:T(8,128)(2,1)S(1)}, u32[]{:S(2)}, u32[]{:S(2)}) async-start(bf16[8,16,1536]{2,1,0:T(8,128)(2,1)} %bitcast.112), calls=%async_computation | async-start | bytes 786432 | tf_op jit(solution)/shard_map/all_to_all | solution.py:318
  72.0 2.7 %collective-permute-start.16 = (bf16[512,512]{1,0:T(8,128)(2,1)S(1)}, bf16[512,512]{1,0:T(8,128)(2,1)S(1)}, u32[]{:S(2)}, u32[]{:S(2)}) collective-permute-start(bf16[512,512]{1,0:T(8,128)(2,1)S(1)} %slice.86), channel_id=1, source_target_pairs={{0,6},{2,0},{4,2},{6,4},{1,7},{3,1},{5,3},{7,5},{8,14},{10,8},{12,... | collective-permute-start | bytes 1572872 | tf_op jit(solution)/shard_map/ppermute | solution.py:25
  74.8 3.2 %collective-permute-start.17 = (bf16[1024,512]{1,0:T(8,128)(2,1)}, bf16[1024,512]{1,0:T(8,128)(2,1)}, u32[]{:S(2)}, u32[]{:S(2)}) collective-permute-start(bf16[1024,512]{1,0:T(8,128)(2,1)} %constant_dynamic-update-slice_fusion.refs_0_), channel_id=1, source_target_pairs={{0,1},{1,0},{2,3},{3,2},{4,5},{5,4},{6,7},{7,6},{8,9},{9,8},{10,11... | collective-permute-start | bytes 3145736 | tf_op jit(solution)/shard_map/ppermute | solution.py:25
  78.5 4.5 %collective-permute-done.14.refs_3_ = bf16[512,512]{1,0:T(8,128)(2,1)S(1)} collective-permute-done((bf16[512,512]{1,0:T(8,128)(2,1)S(1)}, bf16[512,512]{1,0:T(8,128)(2,1)S(1)}, u32[]{:S(2)}, u32[]{:S(2)}) %collective-permute-start.14) | collective-permute-done | bytes 524320 | tf_op jit(solution)/shard_map/ppermute | solution.py:25
  83.0 5.7 %all-to-all-done = bf16[8,16,1536]{2,1,0:T(8,128)(2,1)S(1)} async-done(((bf16[8,16,1536]{2,1,0:T(8,128)(2,1)}), bf16[8,16,1536]{2,1,0:T(8,128)(2,1)S(1)}, u32[]{:S(2)}, u32[]{:S(2)}) %all-to-all-start) | async-done | bytes 393248 | tf_op jit(solution)/shard_map/all_to_all | solution.py:318
  88.8 3.2 %collective-permute-start.20 = (bf16[512,512]{1,0:T(8,128)(2,1)S(1)}, bf16[512,512]{1,0:T(8,128)(2,1)}, u32[]{:S(2)}, u32[]{:S(2)}) collective-permute-start(bf16[512,512]{1,0:T(8,128)(2,1)S(1)} %collective-permute-done.14.refs_3_), channel_id=1, source_target_pairs={{0,1},{1,0},{2,3},{3,2},{4,5},{5,4},{6,7},{7,6},{8,9},{9,8},{10,11... | collective-permute-start | bytes 1572872 | tf_op jit(solution)/shard_map/ppermute | solution.py:25
  93.5 3.5 %all-to-all-start.1 = ((bf16[8,16,1536]{2,1,0:T(8,128)(2,1)}), bf16[8,16,1536]{2,1,0:T(8,128)(2,1)S(1)}, u32[]{:S(2)}, u32[]{:S(2)}) async-start(bf16[8,16,1536]{2,1,0:T(8,128)(2,1)} %broadcast_in_dim.2), calls=%async_computation.1 | async-start | bytes 786432 | tf_op jit(solution)/shard_map/all_to_all | solution.py:328
  97.3 11.1 %shard_map.94 = (bf16[1024,4096]{1,0:T(8,128)(2,1)}, bf16[512,512]{1,0:T(8,128)(2,1)S(1)}) custom-call(s32[8]{0:T(128)S(1)} %stack.134.blocks_ref, s32[32]{0:T(128)S(1)} %stack.167.places_ref, bf16[1024,512]{1,0:T(8,128)(2,1)} %constant_dynamic-update-slice_fusion.refs_0_, bf16[1024,512]{1,0:T(8,128)(2,1)S(1)} %collective-permute-done.13.refs_1_, ...), custom_call_target="tpu_custom_call" | custom-call | flops 2147483648 | bytes 20971520 | tf_op jit(solution)/shard_map/pallas_call | solution.py:94
  108.6 7.3 %all-to-all-done.1 = bf16[8,16,1536]{2,1,0:T(8,128)(2,1)S(1)} async-done(((bf16[8,16,1536]{2,1,0:T(8,128)(2,1)}), bf16[8,16,1536]{2,1,0:T(8,128)(2,1)S(1)}, u32[]{:S(2)}, u32[]{:S(2)}) %all-to-all-start.1) | async-done | bytes 393248 | tf_op jit(solution)/shard_map/all_to_all | solution.py:328
  115.9 3.3 %collective-permute-start.23 = (bf16[128,1536]{1,0:T(8,128)(2,1)S(1)}, bf16[128,1536]{1,0:T(8,128)(2,1)S(1)}, u32[]{:S(2)}, u32[]{:S(2)}) collective-permute-start(bf16[128,1536]{1,0:T(8,128)(2,1)S(1)} %bitcast.82), channel_id=1, source_target_pairs={{0,192},{64,128},{128,64},{192,0},{1,193},{65,129},{129,65},{193,1... | collective-permute-start | bytes 1179656 | tf_op jit(solution)/shard_map/ppermute | solution.py:43
  119.2 3.5 %all-gather.3.cloned.1.call-done = bf16[88,256,128]{2,1,0:T(8,128)(2,1)} async-done(((bf16[11,256,128]{2,1,0:T(8,128)(2,1)}), bf16[88,256,128]{2,1,0:T(8,128)(2,1)}) %all-gather.3.cloned.1.call-update) | async-done | bytes 5767184 | tf_op jit(solution)/shard_map/all_gather | solution.py:295
  125.1 5.1 %shard_map.95 = bf16[512,512]{1,0:T(8,128)(2,1)S(1)} custom-call(s32[1]{0:T(128)} %constant.92.clone.1.part_ref, bf16[1024,4096]{1,0:T(8,128)(2,1)} %get-tuple-element.57.left_ref, bf16[8,11,256,128]{3,2,1,0:T(8,128)(2,1)} %bitcast.86, bf16[8,11,256,128]{3,2,1,0:T(8,128)(2,1)} %bitcast.87, bf16[8,11,256,128]{3,2,1,0:T(8,128)(2,1)} %bitcast.88, ...), custom_call_target="tpu_custom_call" | custom-call | flops 2147483648 | bytes 9437184 | tf_op jit(solution)/shard_map/pallas_call | solution.py:153
  132.4 5.2 %shard_map.96.own_one = f32[512,512]{1,0:T(8,128)S(1)} custom-call(s32[1]{0:T(128)} %constant.100.clone.1.part_ref, bf16[1024,4096]{1,0:T(8,128)(2,1)} %get-tuple-element.57.left_ref, bf16[8,11,256,128]{3,2,1,0:T(8,128)(2,1)} %bitcast.96, bf16[8,11,256,128]{3,2,1,0:T(8,128)(2,1)} %bitcast.95, bf16[8,11,256,128]{3,2,1,0:T(8,128)(2,1)} %bitcast.94, ...), custom_call_target="tpu_custom_call" | custom-call | flops 2147483648 | bytes 9437184 | tf_op jit(solution)/shard_map/pallas_call | solution.py:153
  137.7 3.5 %shard_map.97 = bf16[512,256]{1,0:T(8,128)(2,1)S(1)} custom-call(s32[1]{0:T(128)} %constant.92.clone.1.part_ref, bf16[1024,4096]{1,0:T(8,128)(2,1)} %get-tuple-element.57.left_ref, bf16[8,11,256,128]{3,2,1,0:T(8,128)(2,1)} %bitcast.102, bf16[8,11,256,128]{3,2,1,0:T(8,128)(2,1)} %bitcast.103, bf16[8,11,256,128]{3,2,1,0:T(8,128)(2,1)} %bitcast.104, ...), custom_call_target="tpu_custom_call" | custom-call | flops 1073741824 | bytes 6815744 | tf_op jit(solution)/shard_map/pallas_call | solution.py:153
  141.1 2.8 %collective-permute-start.24 = (bf16[512,256]{1,0:T(8,128)(2,1)S(1)}, bf16[512,256]{1,0:T(8,128)(2,1)S(1)}, u32[]{:S(2)}, u32[]{:S(2)}) collective-permute-start(bf16[512,256]{1,0:T(8,128)(2,1)S(1)} %shard_map.97), channel_id=1, source_target_pairs={{0,192},{64,128},{128,64},{192,0},{1,193},{65,129},{129,65},{193,1... | collective-permute-start | bytes 786440 | tf_op jit(solution)/shard_map/ppermute | solution.py:43
  143.9 3.5 %shard_map.98.own_two = f32[512,256]{1,0:T(8,128)S(1)} custom-call(s32[1]{0:T(128)} %constant.100.clone.1.part_ref, bf16[1024,4096]{1,0:T(8,128)(2,1)} %get-tuple-element.57.left_ref, bf16[8,11,256,128]{3,2,1,0:T(8,128)(2,1)} %bitcast.105, bf16[8,11,256,128]{3,2,1,0:T(8,128)(2,1)} %bitcast.106, bf16[8,11,256,128]{3,2,1,0:T(8,128)(2,1)} %bitcast.107, ...), custom_call_target="tpu_custom_call" | custom-call | flops 1073741824 | bytes 6815744 | tf_op jit(solution)/shard_map/pallas_call | solution.py:153
  147.4 2.2 %shard_map.99.refs_4_ = bf16[512,1536]{1,0:T(8,128)(2,1)} custom-call(s32[1]{0:T(128)} %bitcast.group_ref, f32[512,512]{1,0:T(8,128)S(1)} %shard_map.96.own_one, f32[512,256]{1,0:T(8,128)S(1)} %shard_map.98.own_two, bf16[512,512]{1,0:T(8,128)(2,1)S(1)} %collective-permute-done.26.sent_one, bf16[512,512]{1,0:T(8,128)(2,1)S(1)} %pad_maximum_fusion.1.low_ref, ...), custom_call_target="tpu_custom_call" | custom-call | flops 671088640 | bytes 4587520 | tf_op jit(solution)/shard_map/pallas_call | solution.py:213
  (84 shorter events, 39.0 us)
Async XLA Ops:
  7.2 115.5 %all-gather.3.cloned.1.call-start = ((), (), s32[]{:S(2)}) async-start(), calls=%async_computation.2 | async-start | bytes 6488064 | tf_op jit(solution)/shard_map/all_gather | solution.py:295
  7.2 10.7 %collective-permute-start = (bf16[256,512]{1,0:T(8,128)(2,1)}, bf16[256,512]{1,0:T(8,128)(2,1)S(1)}, u32[]{:S(2)}, u32[]{:S(2)}) collective-permute-start(bf16[256,512]{1,0:T(8,128)(2,1)} %param.7), channel_id=1, source_target_pairs={{0,2},{2,4},{4,6},{6,0},{1,3},{3,5},{5,7},{7,1},{8,10},{10,12},{12... | collective-permute-start | bytes 786440 | tf_op jit(solution)/shard_map/ppermute | solution.py:25
  9.3 8.6 %collective-permute-start.1 = (bf16[256,512]{1,0:T(8,128)(2,1)}, bf16[256,512]{1,0:T(8,128)(2,1)S(1)}, u32[]{:S(2)}, u32[]{:S(2)}) collective-permute-start(bf16[256,512]{1,0:T(8,128)(2,1)} %param.7), channel_id=1, source_target_pairs={{0,6},{2,0},{4,2},{6,4},{1,7},{3,1},{5,3},{7,5},{8,14},{10,8},{12,... | collective-permute-start | bytes 786440 | tf_op jit(solution)/shard_map/ppermute | solution.py:25
  14.9 15.0 %collective-permute-start.5 = (bf16[512,512]{1,0:T(8,128)(2,1)}, bf16[512,512]{1,0:T(8,128)(2,1)S(1)}, u32[]{:S(2)}, u32[]{:S(2)}) collective-permute-start(bf16[512,512]{1,0:T(8,128)(2,1)} %param.13), channel_id=1, source_target_pairs={{0,192},{64,128},{128,64},{192,0},{1,193},{65,129},{129,65},{193,1... | collective-permute-start | bytes 1572872 | tf_op jit(solution)/shard_map/ppermute | solution.py:43
  18.0 12.6 %collective-permute-start.6 = (bf16[5,256,128]{1,2,0:T(8,128)(2,1)S(1)}, bf16[5,256,128]{1,2,0:T(8,128)(2,1)S(1)}, u32[]{:S(2)}, u32[]{:S(2)}) collective-permute-start(bf16[5,256,128]{1,2,0:T(8,128)(2,1)S(1)} %pad_maximum_fusion.4), channel_id=1, source_target_pairs={{0,64},{64,0},{128,192},{192,128},{1,65},{65,1},{129,193},{193,129... | collective-permute-start | bytes 983048 | tf_op jit(solution)/shard_map/ppermute | solution.py:47
  39.8 7.4 %collective-permute-start.10 = (bf16[64,1536]{1,0:T(8,128)(2,1)S(1)}, bf16[64,1536]{1,0:T(8,128)(2,1)S(1)}, u32[]{:S(2)}, u32[]{:S(2)}) collective-permute-start(bf16[64,1536]{1,0:T(8,128)(2,1)S(1)} %get-tuple-element.67), channel_id=1, source_target_pairs={{0,192},{64,0},{128,64},{192,128},{1,193},{65,1},{129,65},{193,129... | collective-permute-start | bytes 589832 | tf_op jit(solution)/shard_map/ppermute | solution.py:25
  44.4 26.4 %collective-permute-start.13 = (bf16[1024,512]{1,0:T(8,128)(2,1)}, bf16[1024,512]{1,0:T(8,128)(2,1)S(1)}, u32[]{:S(2)}, u32[]{:S(2)}) collective-permute-start(bf16[1024,512]{1,0:T(8,128)(2,1)} %constant_dynamic-update-slice_fusion.refs_0_), channel_id=1, source_target_pairs={{0,2},{2,4},{4,6},{6,0},{1,3},{3,5},{5,7},{7,1},{8,10},{10,12},{12... | collective-permute-start | bytes 3145736 | tf_op jit(solution)/shard_map/ppermute | solution.py:25
  44.4 26.5 %collective-permute-start.15 = (bf16[1024,512]{1,0:T(8,128)(2,1)}, bf16[1024,512]{1,0:T(8,128)(2,1)}, u32[]{:S(2)}, u32[]{:S(2)}) collective-permute-start(bf16[1024,512]{1,0:T(8,128)(2,1)} %constant_dynamic-update-slice_fusion.refs_0_), channel_id=1, source_target_pairs={{0,6},{2,0},{4,2},{6,4},{1,7},{3,1},{5,3},{7,5},{8,14},{10,8},{12,... | collective-permute-start | bytes 3145736 | tf_op jit(solution)/shard_map/ppermute | solution.py:25
  49.6 10.6 %collective-permute-start.11 = (bf16[128,1536]{1,0:T(8,128)(2,1)}, bf16[128,1536]{1,0:T(8,128)(2,1)}, u32[]{:S(2)}, u32[]{:S(2)}) collective-permute-start(bf16[128,1536]{1,0:T(8,128)(2,1)} %pad_maximum_fusion.2), channel_id=1, source_target_pairs={{0,64},{64,128},{128,192},{192,0},{1,65},{65,129},{129,193},{193,1... | collective-permute-start | bytes 1179656 | tf_op jit(solution)/shard_map/ppermute | solution.py:25
  50.4 9.8 %collective-permute-start.12 = (bf16[128,1536]{1,0:T(8,128)(2,1)}, bf16[128,1536]{1,0:T(8,128)(2,1)}, u32[]{:S(2)}, u32[]{:S(2)}) collective-permute-start(bf16[128,1536]{1,0:T(8,128)(2,1)} %pad_maximum_fusion.3), channel_id=1, source_target_pairs={{0,192},{64,0},{128,64},{192,128},{1,193},{65,1},{129,65},{193,129... | collective-permute-start | bytes 1179656 | tf_op jit(solution)/shard_map/ppermute | solution.py:25
  62.3 26.5 %all-to-all-start = ((bf16[8,16,1536]{2,1,0:T(8,128)(2,1)}), bf16[8,16,1536]{2,1,0:T(8,128)(2,1)S(1)}, u32[]{:S(2)}, u32[]{:S(2)}) async-start(bf16[8,16,1536]{2,1,0:T(8,128)(2,1)} %bitcast.112), calls=%async_computation | async-start | bytes 786432 | tf_op jit(solution)/shard_map/all_to_all | solution.py:318
  70.8 12.1 %collective-permute-start.14 = (bf16[512,512]{1,0:T(8,128)(2,1)S(1)}, bf16[512,512]{1,0:T(8,128)(2,1)S(1)}, u32[]{:S(2)}, u32[]{:S(2)}) collective-permute-start(bf16[512,512]{1,0:T(8,128)(2,1)S(1)} %slice.85), channel_id=1, source_target_pairs={{0,2},{2,4},{4,6},{6,0},{1,3},{3,5},{5,7},{7,1},{8,10},{10,12},{12... | collective-permute-start | bytes 1572872 | tf_op jit(solution)/shard_map/ppermute | solution.py:25
  72.0 11.0 %collective-permute-start.16 = (bf16[512,512]{1,0:T(8,128)(2,1)S(1)}, bf16[512,512]{1,0:T(8,128)(2,1)S(1)}, u32[]{:S(2)}, u32[]{:S(2)}) collective-permute-start(bf16[512,512]{1,0:T(8,128)(2,1)S(1)} %slice.86), channel_id=1, source_target_pairs={{0,6},{2,0},{4,2},{6,4},{1,7},{3,1},{5,3},{7,5},{8,14},{10,8},{12,... | collective-permute-start | bytes 1572872 | tf_op jit(solution)/shard_map/ppermute | solution.py:25
  74.8 22.5 %collective-permute-start.17 = (bf16[1024,512]{1,0:T(8,128)(2,1)}, bf16[1024,512]{1,0:T(8,128)(2,1)}, u32[]{:S(2)}, u32[]{:S(2)}) collective-permute-start(bf16[1024,512]{1,0:T(8,128)(2,1)} %constant_dynamic-update-slice_fusion.refs_0_), channel_id=1, source_target_pairs={{0,1},{1,0},{2,3},{3,2},{4,5},{5,4},{6,7},{7,6},{8,9},{9,8},{10,11... | collective-permute-start | bytes 3145736 | tf_op jit(solution)/shard_map/ppermute | solution.py:25
  78.0 19.3 %collective-permute-start.18 = (bf16[1024,512]{1,0:T(8,128)(2,1)S(1)}, bf16[1024,512]{1,0:T(8,128)(2,1)}, u32[]{:S(2)}, u32[]{:S(2)}) collective-permute-start(bf16[1024,512]{1,0:T(8,128)(2,1)S(1)} %collective-permute-done.13.refs_1_), channel_id=1, source_target_pairs={{0,1},{1,0},{2,3},{3,2},{4,5},{5,4},{6,7},{7,6},{8,9},{9,8},{10,11... | collective-permute-start | bytes 3145736 | tf_op jit(solution)/shard_map/ppermute | solution.py:25
  78.0 19.3 %collective-permute-start.19 = (bf16[1024,512]{1,0:T(8,128)(2,1)}, bf16[1024,512]{1,0:T(8,128)(2,1)}, u32[]{:S(2)}, u32[]{:S(2)}) collective-permute-start(bf16[1024,512]{1,0:T(8,128)(2,1)} %collective-permute-done.15.refs_2_), channel_id=1, source_target_pairs={{0,1},{1,0},{2,3},{3,2},{4,5},{5,4},{6,7},{7,6},{8,9},{9,8},{10,11... | collective-permute-start | bytes 3145736 | tf_op jit(solution)/shard_map/ppermute | solution.py:25
  88.8 8.5 %collective-permute-start.20 = (bf16[512,512]{1,0:T(8,128)(2,1)S(1)}, bf16[512,512]{1,0:T(8,128)(2,1)}, u32[]{:S(2)}, u32[]{:S(2)}) collective-permute-start(bf16[512,512]{1,0:T(8,128)(2,1)S(1)} %collective-permute-done.14.refs_3_), channel_id=1, source_target_pairs={{0,1},{1,0},{2,3},{3,2},{4,5},{5,4},{6,7},{7,6},{8,9},{9,8},{10,11... | collective-permute-start | bytes 1572872 | tf_op jit(solution)/shard_map/ppermute | solution.py:25
  93.5 22.4 %all-to-all-start.1 = ((bf16[8,16,1536]{2,1,0:T(8,128)(2,1)}), bf16[8,16,1536]{2,1,0:T(8,128)(2,1)S(1)}, u32[]{:S(2)}, u32[]{:S(2)}) async-start(bf16[8,16,1536]{2,1,0:T(8,128)(2,1)} %broadcast_in_dim.2), calls=%async_computation.1 | async-start | bytes 786432 | tf_op jit(solution)/shard_map/all_to_all | solution.py:328
  115.8 14.4 %collective-permute-start.22 = (bf16[128,1536]{1,0:T(8,128)(2,1)S(1)}, bf16[128,1536]{1,0:T(8,128)(2,1)S(1)}, u32[]{:S(2)}, u32[]{:S(2)}) collective-permute-start(bf16[128,1536]{1,0:T(8,128)(2,1)S(1)} %bitcast.81), channel_id=1, source_target_pairs={{0,64},{64,0},{128,192},{192,128},{1,65},{65,1},{129,193},{193,129... | collective-permute-start | bytes 1179656 | tf_op jit(solution)/shard_map/ppermute | solution.py:47
  115.9 14.4 %collective-permute-start.23 = (bf16[128,1536]{1,0:T(8,128)(2,1)S(1)}, bf16[128,1536]{1,0:T(8,128)(2,1)S(1)}, u32[]{:S(2)}, u32[]{:S(2)}) collective-permute-start(bf16[128,1536]{1,0:T(8,128)(2,1)S(1)} %bitcast.82), channel_id=1, source_target_pairs={{0,192},{64,128},{128,64},{192,0},{1,193},{65,129},{129,65},{193,1... | collective-permute-start | bytes 1179656 | tf_op jit(solution)/shard_map/ppermute | solution.py:43
  123.8 13.9 %collective-permute-start.7 = (bf16[8,256,128]{2,1,0:T(8,128)(2,1)S(1)}, bf16[8,256,128]{2,1,0:T(8,128)(2,1)S(1)}, u32[]{:S(2)}, u32[]{:S(2)}) collective-permute-start(bf16[8,256,128]{2,1,0:T(8,128)(2,1)S(1)} %slice_bitcast_fusion), channel_id=1, source_target_pairs={{0,64},{64,0},{128,192},{192,128},{1,65},{65,1},{129,193},{193,129... | collective-permute-start | bytes 1572872 | tf_op jit(solution)/shard_map/ppermute | solution.py:47
  130.2 17.2 %collective-permute-start.26 = (bf16[512,512]{1,0:T(8,128)(2,1)S(1)}, bf16[512,512]{1,0:T(8,128)(2,1)S(1)}, u32[]{:S(2)}, u32[]{:S(2)}) collective-permute-start(bf16[512,512]{1,0:T(8,128)(2,1)S(1)} %shard_map.95), channel_id=1, source_target_pairs={{0,192},{64,128},{128,64},{192,0},{1,193},{65,129},{129,65},{193,1... | collective-permute-start | bytes 1572872 | tf_op jit(solution)/shard_map/ppermute | solution.py:43
  132.1 15.3 %collective-permute-start.25 = (bf16[128,1536]{1,0:T(8,128)(2,1)S(1)}, bf16[128,1536]{1,0:T(8,128)(2,1)S(1)}, u32[]{:S(2)}, u32[]{:S(2)}) collective-permute-start(bf16[128,1536]{1,0:T(8,128)(2,1)S(1)} %collective-permute-done.23.refs_2_), channel_id=1, source_target_pairs={{0,64},{64,0},{128,192},{192,128},{1,65},{65,1},{129,193},{193,129... | collective-permute-start | bytes 1179656 | tf_op jit(solution)/shard_map/ppermute | solution.py:47
  141.1 8.5 %collective-permute-start.24 = (bf16[512,256]{1,0:T(8,128)(2,1)S(1)}, bf16[512,256]{1,0:T(8,128)(2,1)S(1)}, u32[]{:S(2)}, u32[]{:S(2)}) collective-permute-start(bf16[512,256]{1,0:T(8,128)(2,1)S(1)} %shard_map.97), channel_id=1, source_target_pairs={{0,192},{64,128},{128,64},{192,0},{1,193},{65,129},{129,65},{193,1... | collective-permute-start | bytes 786440 | tf_op jit(solution)/shard_map/ppermute | solution.py:43
  (11 other events, 146.4 us)
Sparse Core Ops, SparseCore 0:
  32.0 90.6 all-gather.2
